TPU v7x, 256 devices: a whole 4x4x8 slice. The times are simulated.
256 devices in a mesh: kv: 64 (over z, y, core), head: 4 (over x).
Axes of the slice: x: 4, y: 4, z: 8, core: 2. Of those that a mesh axis runs over, the one named last changes fastest.
Arguments:
- queries: bfloat16 [64, 128, 576], P('kv', 'head'), may hold values from -512 to 512
- prompt_cache: bfloat16 [2, 65536, 576], P(None, 'kv'), may hold values from -6 to 6
- suffix_cache: bfloat16 [64, 2048, 576], P(None, 'kv'), may hold values from -6 to 6
- prompt_ids: int32 [64], replicated, may hold values from 0 to 1, as said below
- suffix_len: int32 [64], replicated, may hold values from 128 to 2048, as said below
- w_uv: bfloat16 [128, 512, 128], P('head'), may hold values from -2.5 to 2.5
- w_out: bfloat16 [16384, 7168], P('head', 'kv'), may hold values from -0.046875 to 0.046875
Outputs:
- mixed: bfloat16 [64, 7168], P(None, ('kv', 'head'))
Inputs may be any that keep to these rules, and one draw needn't show every extreme that they name: `prompt_ids`: each prompt id is used by exactly 32 rows. `suffix_len`: every length is a whole number of blocks of 128; some row reaches 2048.
All inputs are finite; a program needn't handle non-finite values.
Results may differ from a plain program's by a relative error of at most 0.01.
Values may be sent and summed in bfloat16 or wider, within the bound.
No kernel may reach another device: no remote copies, remote signals or barrier semaphores. Data moves between devices by JAX's collectives and lax.ppermute only.
A program may use at most 128 MiB of HBM per device.

v0:
```python
import jax
import jax.numpy as jnp
from jax import lax
from jax.sharding import PartitionSpec as P

ROPE = 64
NOPE = 128


def global_top(peak_here):
    return lax.pmax(peak_here, "kv")


def per_device(queries, prompt_cache, suffix_cache, prompt_ids, suffix_len, w_uv, w_out):
    score_scale = (NOPE + ROPE) ** (-0.5)
    gathered = lax.all_gather(queries, "kv", axis=0, tiled=True)
    row_count = gathered.shape[0]
    head_count = gathered.shape[1]
    prompt_count = prompt_cache.shape[0]
    latent_width = w_uv.shape[1]
    latent_prompt = prompt_cache[:, :, :latent_width]
    suffix_scores = (
        jnp.einsum("rhe,rte->rht", gathered, suffix_cache, preferred_element_type=jnp.float32)
        * score_scale
    )
    suffix_local = suffix_cache.shape[1]
    position = lax.axis_index("kv") * suffix_local + jnp.arange(suffix_local, dtype=jnp.int32)
    allowed = (position[None, :] < suffix_len[:, None])[:, None, :]
    suffix_peak = jnp.where(allowed, suffix_scores, -jnp.inf).max(-1)
    prompt_scores = []
    prefix_peak = jnp.full((row_count, head_count), -jnp.inf, jnp.float32)
    for k in range(prompt_count):
        scores_here = (
            jnp.einsum("rhe,te->rht", gathered, prompt_cache[k], preferred_element_type=jnp.float32)
            * score_scale
        )
        chosen = (prompt_ids == k)[:, None]
        prefix_peak = jnp.maximum(prefix_peak, jnp.where(chosen, scores_here.max(-1), -jnp.inf))
        prompt_scores.append(scores_here)
    peak_here = jnp.maximum(prefix_peak, suffix_peak)
    shift = global_top(peak_here)
    suffix_weights = jnp.where(allowed, jnp.exp(suffix_scores - shift[:, :, None]), 0.0)
    denominator = suffix_weights.sum(-1)
    latent_part = jnp.einsum(
        "rht,rtl->rhl",
        suffix_weights.astype(jnp.bfloat16),
        suffix_cache[:, :, :latent_width],
        preferred_element_type=jnp.float32,
    )
    for k in range(prompt_count):
        chosen = (prompt_ids == k)[:, None, None]
        weights_here = jnp.where(chosen, jnp.exp(prompt_scores[k] - shift[:, :, None]), 0.0)
        denominator = denominator + weights_here.sum(-1)
        latent_part = latent_part + jnp.einsum(
            "rht,tl->rhl",
            weights_here.astype(jnp.bfloat16),
            latent_prompt[k],
            preferred_element_type=jnp.float32,
        )
    share_width = latent_width // lax.axis_size("kv")
    latent_start = lax.axis_index("kv") * share_width
    latent_share = lax.psum_scatter(latent_part, "kv", scatter_dimension=2, tiled=True)
    denominator_all = lax.psum(denominator, "kv")
    attended = latent_share / denominator_all[:, :, None]
    uv_slice = lax.dynamic_slice_in_dim(w_uv, latent_start, share_width, 1).astype(jnp.float32)
    value_part = jnp.einsum("rhl,hlv->rhv", attended, uv_slice, precision=lax.Precision.HIGHEST)
    head_values = lax.psum(value_part, "kv").astype(jnp.bfloat16)
    flat_values = head_values.reshape(row_count, head_count * head_values.shape[2])
    partial_output = jnp.dot(flat_values, w_out, preferred_element_type=jnp.float32)
    return lax.psum_scatter(partial_output, "head", scatter_dimension=1, tiled=True).astype(
        jnp.bfloat16
    )


def solution(mesh):
    placed = (
        P("kv", "head", None),
        P(None, "kv", None),
        P(None, "kv", None),
        P(),
        P(),
        P("head", None, None),
        P("head", "kv"),
    )
    return jax.shard_map(
        per_device, mesh=mesh, in_specs=placed, out_specs=P(None, ("kv", "head")), check_vma=False
    )
```

profile of v0, /device:TPU:1, one launch (start us, length us, event | category | flops | bytes accessed | tf_op | source)
XLA Modules:
  0.0 922.0 jit_solution(10292816772770659231)
XLA Ops:
  6.5 0.0 copy-start
  6.5 0.0 all-gather.2.cloned.1.call-start
  6.5 0.7 all-gather.2.cloned.1.call-update
  7.3 0.0 reduce-scatter.4.cloned.1.call-start
  7.3 0.7 broadcast_compare_fusion.2
  8.0 0.7 broadcast_compare_fusion
  8.7 83.4 %all-gather.2.cloned.1.call-done = bf16[64,32,576]{2,1,0:T(8,128)(2,1)} async-done(((bf16[1,32,576]{2,1,0:T(8,128)(2,1)}), bf16[64,32,576]{2,1,0:T(8,128)(2,1)}) %all-gather.2.cloned.1.call-update) | async-done | bytes 2359312 | tf_op jit(solution)/shard_map/all_gather | solution.py:16
  92.1 3.5 fusion.40
  95.6 0.8 copy.40
  96.4 0.1 select_reduce_fusion
  96.5 0.1 copy.41
  96.6 0.0 copy-start.11
  96.6 8.9 multiply_reduce_fusion
  105.5 0.0 copy-done.2
  105.5 0.0 copy-done.11
  105.5 5.7 multiply_reduce_fusion.1
  111.1 0.0 copy-done.7
  111.1 0.1 maximum_maximum_fusion
  111.2 243.3 %pmax.7 = f32[64,32]{1,0:T(8,128)S(1)} all-reduce(f32[64,32]{1,0:T(8,128)S(1)} %maximum_maximum_fusion), channel_id=1, replica_groups=mesh['kv'=64,'head'=4] {'kv'}, use_global_device_ids=true, to_apply=%region_3.4 | all-reduce | flops 2048 | bytes 16384 | tf_op jit(solution)/shard_map/pmax | solution.py:11
  354.5 0.1 copy.42
  354.6 0.9 fusion.31
  355.5 0.0 copy-done.5
  355.5 8.6 fusion.7
  364.1 0.0 copy-done.3
  364.1 0.0 slice-done
  364.1 0.0 copy-start.1
  364.1 5.4 fusion.5
  369.5 2.5 copy.43
  372.0 6.3 add_add_fusion
  378.3 9.2 copy.49
  387.4 0.0 reduce-scatter.4.cloned.1.call-update
  387.5 0.1 copy.59
  387.5 0.6 copy-done.4
  388.2 0.0 copy-done.6
  388.2 7.8 fusion.1
  396.0 246.8 %psum.14 = f32[64,32]{1,0:T(8,128)S(1)} all-reduce(f32[64,32]{1,0:T(8,128)S(1)} %add_add_fusion.1), channel_id=1, replica_groups=mesh['kv'=64,'head'=4] {'kv'}, use_global_device_ids=true, to_apply=%region_8.9 | all-reduce | flops 2048 | bytes 16384 | tf_op jit(solution)/shard_map/psum | solution.py:63
  642.7 0.1 copy.51
  642.8 0.9 broadcast_divide_fusion
  643.7 1.9 convolution_bitcast_fusion
  645.6 254.8 %all-reduce.3 = bf16[64,32,128]{2,0,1:T(8,128)(2,1)S(1)} all-reduce(f32[64,32,128]{2,0,1:T(8,128)S(1)} %convolution_bitcast_fusion), channel_id=1, replica_groups=mesh['kv'=64,'head'=4] {'kv'}, use_global_device_ids=true, to_apply=%region_9.10 | all-reduce | flops 262144 | bytes 1572864 | tf_op jit(solution)/shard_map/psum | solution.py:67
  900.4 0.0 copy-done
  900.5 0.4 fusion.28
  900.9 9.6 %fusion = f32[64,32]{0,1:T(8,128)S(1)} fusion(f32[64,112]{0,1:T(8,128)S(1)} %fusion.28), kind=kCustom, calls=%all-reduce-scatter | all-reduce-scatter fusion | flops 8193 | bytes 37888
  910.5 2.6 collective-permute-start
  913.1 0.6 dynamic-slice.4
  914.3 0.0 collective-permute-done
  914.4 0.2 concatenate
  914.5 0.6 dynamic-slice_convert_fusion
  (21 shorter events, 0.0 us)
Async XLA Ops:
  6.5 893.9 %copy-start = (bf16[4096,112]{0,1:T(8,128)(2,1)S(1)}, bf16[4096,112]{0,1:T(8,128)(2,1)}, u32[]{:S(2)}) copy-start(bf16[4096,112]{0,1:T(8,128)(2,1)} %param.13) | copy-start | bytes 2752516
  6.5 85.6 %all-gather.2.cloned.1.call-start = ((), (), s32[]{:S(2)}) async-start(), calls=%async_computation.1 | async-start | bytes 2662400 | tf_op jit(solution)/shard_map/all_gather | solution.py:16
  7.3 635.5 %reduce-scatter.4.cloned.1.call-start = ((), (), s32[]{:S(2)}) async-start(), calls=%async_computation.2 | async-start | bytes 8519680 | tf_op jit(solution)/shard_map/reduce_scatter | solution.py:62
  8.0 103.1 %copy-start.7 = (pred[64]{0:T(512)(128)(4,1)}, pred[64]{0:T(512)(128)(4,1)S(1)}, u32[]{:S(2)}) copy-start(pred[64]{0:T(512)(128)(4,1)S(1)} %get-tuple-element.10) | copy-start | bytes 196
  8.0 347.5 %copy-start.5 = (pred[64]{0:T(512)(128)(4,1)}, pred[64]{0:T(512)(128)(4,1)S(1)}, u32[]{:S(2)}) copy-start(pred[64]{0:T(512)(128)(4,1)S(1)} %get-tuple-element.9) | copy-start | bytes 196
  96.6 8.9 copy-start.2
  96.6 8.9 copy-start.11
  354.5 9.5 %copy-start.3 = (f32[64,32]{1,0:T(8,128)}, f32[64,32]{1,0:T(8,128)S(1)}, u32[]{:S(2)}) copy-start(f32[64,32]{1,0:T(8,128)S(1)} %pmax.7) | copy-start | bytes 24580
  354.6 9.5 %slice-start = ((s8[8388608]{0:T(1024)(128)(4,1)}), s8[4194304]{0:T(1024)(128)(4,1)S(1)}, s32[]{:S(2)}) async-start(s8[8388608]{0:T(1024)(128)(4,1)} %bitcast.40), calls=%async_computation.3 | async-start | bytes 8388608
  355.5 8.6 slice-start.1
  355.5 8.6 copy-start.8
  364.1 7.9 copy-start.1
  387.4 0.8 copy-start.4
  387.4 0.8 copy-start.6
  387.4 0.8 copy-start.9
  396.0 517.1 %copy-start.10 = (u32[256]{0:T(256)S(1)}, u32[256]{0:T(256)}, u32[]{:S(2)}) copy-start(u32[256]{0:T(256)} %constant.30) | copy-start | bytes 3076
  910.5 3.9 collective-permute-start
Sparse Core Ops, SparseCore 0:
  10.1 81.9 all-gather.1
  387.6 149.2 reduce-scatter.3
where the time goes:
time: 930 us; the launch traced here: 922 us
  blocking collectives  755 us (81%)
  waiting for transfers between devices  84.1 us (9%)
  matrix products  40.5 us (4%)
  local copies, waits for them, and re-layouts  14.8 us (2%)
  between operations  14.2 us (2%)
  other arithmetic  11.2 us (1%)
    psum x1, blocking collectives, per_device(): head_values = lax.psum(value_part, 'kv').astype(jnp.bfloat16)  255 us
    psum x1, blocking collectives, per_device(): denominator_all = lax.psum(denominator, 'kv')  247 us
    pmax x1, blocking collectives, global_top(): return lax.pmax(peak_here, 'kv')  243 us
    all_gather x1, waiting for transfers between devices, per_device(): gathered = lax.all_gather(queries, 'kv', axis=0, tiled=True)  83.4 us
  transfers between devices with their start and end apart: 3, of which 1 were waited for; matrix products, arithmetic and copies ran while one was open for 1% of the time, Pallas kernels for 0%

commit v1 on v0

v1 whole, which is shorter than its diff:
```python
import jax
import jax.numpy as jnp
from jax import lax
from jax.experimental import pallas as pl
from jax.experimental.pallas import tpu as pltpu
from jax.sharding import Mesh, PartitionSpec as P

ROPE = 64
NOPE = 128
SCALE = (NOPE + ROPE) ** (-0.5)
NZ, NY, NC, NX = 8, 4, 2, 4
ROWS = 64
GROUP = 16
LAT = 512
VH = 128
MASKED = -1e30
VMEM = 56 * 1024 * 1024


def nt_dot(a, b):
    return lax.dot_general(a, b, (((1,), (1,)), ((), ())), preferred_element_type=jnp.float32)


def attend_kernel(
    place_ref, ids_ref, len_ref, q0_ref, q1_ref, q2_ref, q3_ref, own_ref, peer_ref,
    suf_own_ref, suf_peer_ref, uv_ref, out_ref,
    sorted_ref, keys_ref, latent_ref, value_ref, stat_ref, row_ref,
):
    z, y, own_base, peer_base = place_ref[0], place_ref[1], place_ref[2], place_ref[3]
    q_refs = (q0_ref, q1_ref, q2_ref, q3_ref)
    counts = [jnp.int32(0), jnp.int32(ROWS // 2)]
    for j in range(NY):
        for k in range(NZ):
            chip = lax.rem(z + NZ - k, NZ) * NY + lax.rem(y + NY - j, NY)
            for b in range(2):
                row = chip * 2 + b
                second = ids_ref[row] != 0
                spot = jnp.where(second, counts[1], counts[0])
                counts = [
                    counts[0] + jnp.where(second, 0, 1),
                    counts[1] + jnp.where(second, 1, 0),
                ]
                row_ref[spot] = row
                sorted_ref[pl.ds(pl.multiple_of(spot * GROUP, GROUP), GROUP), :] = q_refs[j][
                    k * 2 + b
                ]
    lane = lax.broadcasted_iota(jnp.int32, (64, 256), 1)
    part = lax.broadcasted_iota(jnp.int32, (64, 256), 0) // GROUP
    inside = lax.rem(lane, 64)
    position = jnp.where(inside < 32, own_base + inside, peer_base + inside - 32)
    same = lane // 64 == part
    block = 256
    for t in range(ROWS * GROUP // block):
        k = t // 2
        q = sorted_ref[pl.ds(t * block, block), :]
        s_own = jnp.dot(q, own_ref[k], preferred_element_type=jnp.float32)
        s_peer = jnp.dot(q, peer_ref[k], preferred_element_type=jnp.float32)
        suffix = []
        for g in range(4):
            group = t * 4 + g
            limit = jnp.zeros((64, 256), jnp.int32)
            for i in range(4):
                row = row_ref[group * 4 + i]
                keys_ref[group, pl.ds(i * 64, 32), :] = suf_own_ref[row]
                keys_ref[group, pl.ds(i * 64 + 32, 32), :] = suf_peer_ref[row]
                limit = jnp.where(part == i, len_ref[row], limit)
            s = nt_dot(q[g * 64:(g + 1) * 64], keys_ref[group])
            suffix.append(jnp.where(jnp.logical_and(same, position < limit), s, MASKED))
        s_suf = jnp.concatenate(suffix, axis=0)
        peak = jnp.maximum(
            jnp.maximum(s_own.max(-1, keepdims=True), s_peer.max(-1, keepdims=True)),
            s_suf.max(-1, keepdims=True),
        )
        w_own = jnp.exp((s_own - peak) * SCALE)
        w_peer = jnp.exp((s_peer - peak) * SCALE)
        w_suf = jnp.exp((s_suf - peak) * SCALE)
        total = (
            w_own.sum(-1, keepdims=True)
            + w_peer.sum(-1, keepdims=True)
            + w_suf.sum(-1, keepdims=True)
        )
        acc = nt_dot(w_own.astype(jnp.bfloat16), own_ref[k, :LAT, :])
        acc = acc + nt_dot(w_peer.astype(jnp.bfloat16), peer_ref[k, :LAT, :])
        w_suf = w_suf.astype(jnp.bfloat16)
        acc = acc + jnp.concatenate(
            [
                jnp.dot(
                    w_suf[g * 64:(g + 1) * 64],
                    keys_ref[t * 4 + g, :, :LAT],
                    preferred_element_type=jnp.float32,
                )
                for g in range(4)
            ],
            axis=0,
        )
        acc = acc / total
        for c in range(LAT // 128):
            latent_ref[c, pl.ds(t * block, block), :] = acc[:, c * 128:(c + 1) * 128]
        mass = peak * SCALE + jnp.log(total)
        for i in range(block // GROUP):
            row = row_ref[t * (block // GROUP) + i]
            stat_ref[pl.ds(pl.multiple_of(row * GROUP, GROUP), GROUP), :] = jnp.broadcast_to(
                mass[i * GROUP:(i + 1) * GROUP], (GROUP, 128)
            )
    for h in range(GROUP):
        rows = jnp.concatenate(
            [latent_ref[c, pl.ds(h, ROWS, stride=GROUP), :] for c in range(LAT // 128)], axis=1
        ).astype(jnp.bfloat16)
        value_ref[pl.ds(h, ROWS, stride=GROUP), :] = jnp.dot(
            rows, uv_ref[h], preferred_element_type=jnp.float32
        )
    for i in range(ROWS):
        row = row_ref[i]
        out_ref[row // 2, lax.rem(row, 2)] = value_ref[pl.ds(i * GROUP, GROUP), :].astype(
            jnp.bfloat16
        )
    diagonal = lax.broadcasted_iota(jnp.int32, (128, 128), 0) == lax.broadcasted_iota(
        jnp.int32, (128, 128), 1
    )
    line = lax.broadcasted_iota(jnp.int32, (GROUP, 128), 0)
    for b in range(ROWS * GROUP // 128):
        mass = jnp.where(diagonal, stat_ref[pl.ds(b * 128, 128), :], 0.0).sum(0, keepdims=True)
        high = mass.astype(jnp.bfloat16).astype(jnp.float32)
        middle = (mass - high).astype(jnp.bfloat16).astype(jnp.float32)
        low = mass - high - middle
        stats = jnp.where(
            line == 0, high, jnp.where(line == 1, middle, jnp.where(line == 2, low, 0.0))
        ).astype(jnp.bfloat16)
        for i in range(4):
            out_ref[b * 4 + i, 2] = stats


def attend(place, ids, lens, qs, own, peer, suf_own, suf_peer, uv):
    smem = pl.BlockSpec(memory_space=pltpu.SMEM)
    vmem = pl.BlockSpec(memory_space=pltpu.VMEM)
    return pl.pallas_call(
        attend_kernel,
        out_shape=jax.ShapeDtypeStruct((NZ * NY, 3, GROUP, VH), jnp.bfloat16),
        in_specs=[smem] * 3 + [vmem] * 9,
        out_specs=vmem,
        scratch_shapes=[
            pltpu.VMEM((ROWS * GROUP, LAT + ROPE), jnp.bfloat16),
            pltpu.VMEM((ROWS // 4, 256, LAT + ROPE), jnp.bfloat16),
            pltpu.VMEM((LAT // 128, ROWS * GROUP, 128), jnp.float32),
            pltpu.VMEM((ROWS * GROUP, VH), jnp.float32),
            pltpu.VMEM((ROWS * GROUP, 128), jnp.float32),
            pltpu.SMEM((ROWS,), jnp.int32),
        ],
        compiler_params=pltpu.CompilerParams(vmem_limit_bytes=VMEM),
        cost_estimate=pl.CostEstimate(
            flops=2 * 1024 * 2200 * 1088, bytes_accessed=14 * 2**20, transcendentals=2 * 2**20
        ),
    )(place, ids, lens, *qs, own, peer, suf_own, suf_peer, uv)


def combine_kernel(place_ref, got_ref, out_ref, turned_ref):
    mass = got_ref[:, 2].astype(jnp.float32).sum(1)
    weight = jnp.exp(mass - mass.max(0, keepdims=True))
    weight = weight / weight.sum(0, keepdims=True)
    turned_ref[...] = jnp.concatenate([weight, jnp.zeros((96, 128), jnp.float32)], axis=0).T
    start = pl.multiple_of(lax.rem(place_ref[1], 4) * 32, 32)
    column = turned_ref[pl.ds(start, 32), :]
    total = jnp.zeros((32, VH), jnp.float32)
    for d in range(NZ * NY):
        part = jnp.concatenate([got_ref[d, 0], got_ref[d, 1]], axis=0).astype(jnp.float32)
        total = total + column[:, d:d + 1] * part
    total = total.astype(jnp.bfloat16)
    for d in range(NZ * NY):
        out_ref[d, 0] = total[:GROUP]
        out_ref[d, 1] = total[GROUP:]


def combine(place, got):
    return pl.pallas_call(
        combine_kernel,
        out_shape=jax.ShapeDtypeStruct((NZ * NY, 2, GROUP, VH), jnp.bfloat16),
        in_specs=[pl.BlockSpec(memory_space=pltpu.SMEM), pl.BlockSpec(memory_space=pltpu.VMEM)],
        out_specs=pl.BlockSpec(memory_space=pltpu.VMEM),
        scratch_shapes=[pltpu.VMEM((128, 128), jnp.float32)],
        compiler_params=pltpu.CompilerParams(vmem_limit_bytes=VMEM),
    )(place, got)


def project_kernel(place_ref, values_ref, own_ref, peer_ref, out_ref, wide_ref):
    core = place_ref[4]
    for r in range(ROWS):
        wide_ref[pl.ds(r * GROUP, GROUP), :] = values_ref[r // 2, r % 2].astype(jnp.float32)
    flat = jnp.concatenate(
        [wide_ref[pl.ds(h, ROWS, stride=GROUP), :].astype(jnp.bfloat16) for h in range(GROUP)],
        axis=1,
    )
    mine = nt_dot(own_ref[...], flat)
    other = nt_dot(peer_ref[...], flat)
    for x in range(NX):
        out_ref[core * NX + x] = mine[x * 32:(x + 1) * 32]
        out_ref[(1 - core) * NX + x] = other[x * 32:(x + 1) * 32]


def project(place, values, own, peer):
    vmem = pl.BlockSpec(memory_space=pltpu.VMEM)
    return pl.pallas_call(
        project_kernel,
        out_shape=jax.ShapeDtypeStruct((NC * NX, 32, ROWS), jnp.float32),
        in_specs=[pl.BlockSpec(memory_space=pltpu.SMEM), vmem, vmem, vmem],
        out_specs=vmem,
        scratch_shapes=[pltpu.VMEM((ROWS * GROUP, VH), jnp.float32)],
        compiler_params=pltpu.CompilerParams(vmem_limit_bytes=VMEM),
    )(place, values, own, peer)


def shift(x, axis, size, by):
    return lax.ppermute(x, axis, [(i, (i + by) % size) for i in range(size)])


def per_device(queries, prompt_cache, suffix_cache, prompt_ids, suffix_len, w_uv, w_out):
    z, y, core = lax.axis_index("z"), lax.axis_index("y"), lax.axis_index("c")
    chip = z * NY + y
    own_base = (chip * 2 + core) * 32
    peer_base = (chip * 2 + 1 - core) * 32
    place = jnp.stack([z, y, own_base, peer_base, core]).astype(jnp.int32)
    mine = lax.all_to_all(queries, "c", 1, 0, tiled=True)
    own = jnp.transpose(prompt_cache, (0, 2, 1))
    peer = shift(own, "c", NC, 1)
    suf_peer = shift(suffix_cache, "c", NC, 1)
    w_t = jnp.pad(w_out.T.reshape(NX, 28, -1), ((0, 0), (0, 4), (0, 0))).reshape(NX * 32, -1)
    width = GROUP * VH
    w_own = lax.dynamic_slice_in_dim(w_t, core * width, width, 1)
    w_peer = shift(lax.dynamic_slice_in_dim(w_t, (1 - core) * width, width, 1), "c", NC, 1)
    uv = lax.dynamic_slice_in_dim(w_uv, core * GROUP, GROUP, 0)
    along_z = jnp.concatenate([mine] + [shift(mine, "z", NZ, k) for k in range(1, NZ)], axis=0)
    qs = [along_z] + [shift(along_z, "y", NY, j) for j in range(1, NY)]
    parts = attend(place, prompt_ids, suffix_len, qs, own, peer, suffix_cache, suf_peer, uv)
    got = lax.all_to_all(parts, ("z", "y"), 0, 0, tiled=True)
    values = lax.all_to_all(combine(place, got), ("z", "y"), 0, 0, tiled=True)
    shares = project(place, values, w_own, w_peer)
    summed = lax.all_to_all(shares, ("c", "x"), 0, 0, tiled=True).sum(0)
    return summed[:28].astype(jnp.bfloat16).T


def solution(mesh):
    whole = ("z", "y", "c", "x")
    kv = ("z", "y", "c")
    split = Mesh(mesh.devices.reshape(NZ, NY, NC, NX), whole)
    placed = (
        P(kv, "x", None),
        P(None, kv, None),
        P(None, kv, None),
        P(),
        P(),
        P("x", None, None),
        P("x", kv),
    )
    return jax.shard_map(
        per_device, mesh=split, in_specs=placed, out_specs=P(None, whole), check_vma=False
    )
```

time: 930 us -> 124 us (0.13)
  blocking collectives: 755 us -> 18.4 us
  waiting for transfers between devices: 84.1 us -> 34.2 us
  matrix products: 40.5 us -> 0 us
  starting transfers between devices: 2.67 us -> 36.7 us
  Pallas kernels: 0 us -> 21 us
  between operations: 14.2 us -> 0.15 us
  other arithmetic: 11.2 us -> 1.69 us
    psum x2 -> x0, blocking collectives: 502 us -> none  [the longest x1 255 us: per_device(): head_values = lax.psum(value_part, 'kv').astype(jnp.bfloat16)]
    pmax x1 -> x0, blocking collectives: 243 us -> none  [global_top(): return lax.pmax(peak_here, 'kv')]
    all_gather x1 -> x0, waiting for transfers between devices: 83.4 us -> none  [per_device(): gathered = lax.all_gather(queries, 'kv', axis=0, tiled=True)]
    dot_general x8 -> x0, matrix products: 40.5 us -> none  [the longest x2 14.5 us: per_device(): jnp.einsum('rhe,te->rht', gathered, prompt_cache[k], preferred_element_ty...]
    ppermute x0 -> x13, starting transfers between devices: none -> 25 us  [shift(): return lax.ppermute(x, axis, [(i, (i + by) % size) for i in range(size)])]
    all_to_all x0 -> x2, waiting for transfers between devices: none -> 21.8 us  [the longest x1 11.4 us: per_device(): got = lax.all_to_all(parts, ('z', 'y'), 0, 0, tiled=True)]
    pallas_call x0 -> x3, Pallas kernels: none -> 21 us  [the longest x1 16.4 us: attend(): pl.pallas_call(attend_kernel, out_shape=jax.ShapeDtypeStruct((NZ * NY, 3,...]
    all_to_all x0 -> x2, blocking collectives: none -> 18.4 us  [the longest x1 12.8 us: per_device(): summed = lax.all_to_all(shares, ('c', 'x'), 0, 0, tiled=True).sum(0)]
  transfers between devices with their start and end apart: 3 -> 15, of which waited for: 1 -> 7; matrix products, arithmetic and copies ran while one was open for 1% -> 6% of each run, Pallas kernels for 0% -> 2%
where the time goes in v1:
time: 124 us; the launch traced here: 123 us
  starting transfers between devices  36.7 us (30%)
  waiting for transfers between devices  34.2 us (28%)
  Pallas kernels  21 us (17%)
  blocking collectives  18.4 us (15%)
  local copies, waits for them, and re-layouts  11 us (9%)
  other arithmetic  1.69 us (1%)
    ppermute x13, starting transfers between devices, shift(): return lax.ppermute(x, axis, [(i, (i + by) % size) for i in range(size)])  25 us
    pallas_call x1, Pallas kernels, attend(): pl.pallas_call(attend_kernel, out_shape=jax.ShapeDtypeStruct((NZ * NY, 3,...  16.4 us
    all_to_all x1, blocking collectives, per_device(): summed = lax.all_to_all(shares, ('c', 'x'), 0, 0, tiled=True).sum(0)  12.8 us
    ppermute x13, waiting for transfers between devices, shift(): return lax.ppermute(x, axis, [(i, (i + by) % size) for i in range(size)])  12.4 us
    all_to_all x1, waiting for transfers between devices, per_device(): got = lax.all_to_all(parts, ('z', 'y'), 0, 0, tiled=True)  11.4 us
    all_to_all x1, waiting for transfers between devices, per_device(): values = lax.all_to_all(combine(place, got), ('z', 'y'), 0, 0, tiled=True)  10.4 us
    all_to_all x1, starting transfers between devices, per_device(): got = lax.all_to_all(parts, ('z', 'y'), 0, 0, tiled=True)  6.73 us
    all_to_all x1, blocking collectives, per_device(): mine = lax.all_to_all(queries, 'c', 1, 0, tiled=True)  5.58 us
  transfers between devices with their start and end apart: 15, of which 7 were waited for; matrix products, arithmetic and copies ran while one was open for 6% of the time, Pallas kernels for 2%

profile of v1, /device:TPU:1, one launch (start us, length us, event | category | flops | bytes accessed | tf_op | source)
XLA Modules:
  0.0 123.2 jit_solution(15097386778658752971)
XLA Ops:
  0.0 3.2 %collective-permute-start.10 = (bf16[2,576,1024]{2,1,0:T(8,128)(2,1)}, bf16[2,576,1024]{2,1,0:T(8,128)(2,1)}, u32[]{:S(2)}, u32[]{:S(2)}) collective-permute-start(bf16[2,576,1024]{2,1,0:T(8,128)(2,1)} %bitcast.27), channel_id=1, source_target_pairs={{0,4},{4,0},{1,5},{5,1},{2,6},{6,2},{3,7},{7,3},{8,12},{12,8},{9,1... | collective-permute-start | bytes 7077896 | tf_op jit(solution)/shard_map/ppermute | solution.py:212
  3.2 0.0 collective-permute-start.11
  3.2 0.8 copy.12
  4.1 0.5 broadcast.2
  4.6 0.9 reduce
  5.5 0.1 reshape.11
  5.6 5.6 %all_to_all.27 = bf16[2,2,4608]{2,1,0:T(2,128)(2,1)S(1)} all-to-all(bf16[2,2,4608]{2,1,0:T(2,128)(2,1)S(1)} %reshape.11), channel_id=1, replica_groups=mesh['z'=8,'y'=4,'c'=2,'x'=4] {'c'}, dimensions={0} | all-to-all | bytes 73728 | tf_op jit(solution)/shard_map/all_to_all | solution.py:221
  11.2 0.1 reshape.12
  11.3 0.1 collective-permute-start
  11.4 2.9 %collective-permute-start.1 = (bf16[2,16,576]{2,1,0:T(8,128)(2,1)S(1)}, bf16[2,16,576]{2,1,0:T(8,128)(2,1)S(1)}, u32[]{:S(2)}, u32[]{:S(2)}) collective-permute-start(bf16[2,16,576]{2,1,0:T(8,128)(2,1)S(1)} %bitcast.20), channel_id=1, source_target_pairs={{0,64},{32,96},{64,128},{96,160},{128,192},{160,224},{192,0},{224,... | collective-permute-start | bytes 110600 | tf_op jit(solution)/shard_map/ppermute | solution.py:212
  14.3 3.8 %collective-permute-start.2 = (bf16[2,16,576]{2,1,0:T(8,128)(2,1)S(1)}, bf16[2,16,576]{2,1,0:T(8,128)(2,1)S(1)}, u32[]{:S(2)}, u32[]{:S(2)}) collective-permute-start(bf16[2,16,576]{2,1,0:T(8,128)(2,1)S(1)} %bitcast.21), channel_id=1, source_target_pairs={{0,96},{32,128},{64,160},{96,192},{128,224},{160,0},{192,32},{224,... | collective-permute-start | bytes 110600 | tf_op jit(solution)/shard_map/ppermute | solution.py:212
  18.1 0.0 collective-permute-done
  18.1 2.6 %collective-permute-start.3 = (bf16[2,16,576]{2,1,0:T(8,128)(2,1)S(1)}, bf16[2,16,576]{2,1,0:T(8,128)(2,1)S(1)}, u32[]{:S(2)}, u32[]{:S(2)}) collective-permute-start(bf16[2,16,576]{2,1,0:T(8,128)(2,1)S(1)} %bitcast.23), channel_id=1, source_target_pairs={{0,128},{32,160},{64,192},{96,224},{128,0},{160,32},{192,64},{224,... | collective-permute-start | bytes 110600 | tf_op jit(solution)/shard_map/ppermute | solution.py:212
  20.6 2.5 %collective-permute-start.4 = (bf16[2,16,576]{2,1,0:T(8,128)(2,1)S(1)}, bf16[2,16,576]{2,1,0:T(8,128)(2,1)S(1)}, u32[]{:S(2)}, u32[]{:S(2)}) collective-permute-start(bf16[2,16,576]{2,1,0:T(8,128)(2,1)S(1)} %bitcast.24), channel_id=1, source_target_pairs={{0,160},{32,192},{64,224},{96,0},{128,32},{160,64},{192,96},{224,1... | collective-permute-start | bytes 110600 | tf_op jit(solution)/shard_map/ppermute | solution.py:212
  23.2 0.0 collective-permute-done.2
  23.2 2.5 %collective-permute-start.5 = (bf16[2,16,576]{2,1,0:T(8,128)(2,1)S(1)}, bf16[2,16,576]{2,1,0:T(8,128)(2,1)S(1)}, u32[]{:S(2)}, u32[]{:S(2)}) collective-permute-start(bf16[2,16,576]{2,1,0:T(8,128)(2,1)S(1)} %bitcast.25), channel_id=1, source_target_pairs={{0,192},{32,224},{64,0},{96,32},{128,64},{160,96},{192,128},{224,1... | collective-permute-start | bytes 110600 | tf_op jit(solution)/shard_map/ppermute | solution.py:212
  25.6 1.3 %collective-permute-start.6 = (bf16[2,16,576]{2,1,0:T(8,128)(2,1)S(1)}, bf16[2,16,576]{2,1,0:T(8,128)(2,1)S(1)}, u32[]{:S(2)}, u32[]{:S(2)}) collective-permute-start(bf16[2,16,576]{2,1,0:T(8,128)(2,1)S(1)} %bitcast.26), channel_id=1, source_target_pairs={{0,224},{32,0},{64,32},{96,64},{128,96},{160,128},{192,160},{224,1... | collective-permute-start | bytes 110600 | tf_op jit(solution)/shard_map/ppermute | solution.py:212
  26.9 2.6 %collective-permute-done.5 = bf16[2,16,576]{2,1,0:T(8,128)(2,1)S(1)} collective-permute-done((bf16[2,16,576]{2,1,0:T(8,128)(2,1)S(1)}, bf16[2,16,576]{2,1,0:T(8,128)(2,1)S(1)}, u32[]{:S(2)}, u32[]{:S(2)}) %collective-permute-start.5) | collective-permute-done | bytes 36896 | tf_op jit(solution)/shard_map/ppermute | solution.py:212
  29.6 0.9 collective-permute-done.6
  30.5 1.4 %collective-permute-start.7 = (bf16[16,16,576]{2,1,0:T(8,128)(2,1)S(1)}, bf16[16,16,576]{2,1,0:T(8,128)(2,1)S(1)}, u32[]{:S(2)}, u32[]{:S(2)}) collective-permute-start(bf16[16,16,576]{2,1,0:T(8,128)(2,1)S(1)} %constant_dynamic-update-slice_fusion.q0_ref), channel_id=1, source_target_pairs={{0,8},{8,16},{16,24},{24,0},{1,9},{9,17},{17,25},{25,1},{2,10},{10... | collective-permute-start | bytes 884744 | tf_op jit(solution)/shard_map/ppermute | solution.py:212
  31.9 2.6 %collective-permute-start.8 = (bf16[16,16,576]{2,1,0:T(8,128)(2,1)S(1)}, bf16[16,16,576]{2,1,0:T(8,128)(2,1)S(1)}, u32[]{:S(2)}, u32[]{:S(2)}) collective-permute-start(bf16[16,16,576]{2,1,0:T(8,128)(2,1)S(1)} %constant_dynamic-update-slice_fusion.q0_ref), channel_id=1, source_target_pairs={{0,16},{8,24},{16,0},{24,8},{1,17},{9,25},{17,1},{25,9},{2,18},{10... | collective-permute-start | bytes 884744 | tf_op jit(solution)/shard_map/ppermute | solution.py:212
  34.5 1.1 collective-permute-start.9
  35.5 0.6 stack.23.place_ref
  36.1 3.2 %constant_dynamic-slice_fusion.2.uv_ref = bf16[16,512,128]{2,1,0:T(8,128)(2,1)} fusion(bf16[32,512,128]{2,1,0:T(8,128)(2,1)} %param.12, s32[]{:T(128)S(6)} %select_n.9), kind=kLoop, calls=%fused_computation.12 | loop fusion | bytes 4194308 | tf_op jit(solution)/shard_map/dynamic_slice | solution.py:229
  39.3 0.4 collective-permute-done.7.q1_ref
  39.6 8.1 %collective-permute-done.8.q2_ref = bf16[16,16,576]{2,1,0:T(8,128)(2,1)S(1)} collective-permute-done((bf16[16,16,576]{2,1,0:T(8,128)(2,1)S(1)}, bf16[16,16,576]{2,1,0:T(8,128)(2,1)S(1)}, u32[]{:S(2)}, u32[]{:S(2)}) %collective-permute-start.8) | collective-permute-done | bytes 294944 | tf_op jit(solution)/shard_map/ppermute | solution.py:212
  47.8 0.4 collective-permute-done.9.q3_ref
  48.2 0.4 copy-done.6
  48.5 0.4 copy-done.7
  48.9 16.4 %shard_map.73 = bf16[32,3,16,128]{3,2,1,0:T(8,128)(2,1)} custom-call(s32[5]{0:T(128)} %stack.23.place_ref, s32[64]{0:T(128)} %ids_ref.1, s32[64]{0:T(128)} %len_ref.1, bf16[16,16,576]{2,1,0:T(8,128)(2,1)} %copy-done.4, bf16[16,16,576]{2,1,0:T(8,128)(2,1)} %copy-done.5, bf16[16,16,576]{2,1,0:T(8,128)(2,1)} %copy-done.6, bf16[16,16,576]{2,1,0:T(8,128)(2,1)} %copy-done.7, ...), custom_call_target="tpu_custom_call" | custom-call | flops 4902092800 | bytes 14680064 | tf_op jit(solution)/shard_map/pallas_call | solution.py:136
  65.3 6.7 %all-to-all-start.1 = ((bf16[32,3,16,128]{3,2,1,0:T(8,128)(2,1)}), bf16[32,3,16,128]{3,2,1,0:T(8,128)(2,1)S(1)}, u32[]{:S(2)}, u32[]{:S(2)}) async-start(bf16[32,3,16,128]{3,2,1,0:T(8,128)(2,1)} %shard_map.73), calls=%async_computation.1 | async-start | bytes 786432 | tf_op jit(solution)/shard_map/all_to_all | solution.py:233
  72.0 0.2 reshape.9
  72.2 0.1 pad.4
  72.4 0.9 constant_dynamic-slice_fusion
  73.2 1.2 collective-permute-start.12
  74.4 11.4 %all-to-all-done.1.got_ref = bf16[32,3,16,128]{3,2,1,0:T(8,128)(2,1)S(1)} async-done(((bf16[32,3,16,128]{3,2,1,0:T(8,128)(2,1)}), bf16[32,3,16,128]{3,2,1,0:T(8,128)(2,1)S(1)}, u32[]{:S(2)}, u32[]{:S(2)}) %all-to-all-start.1) | async-done | bytes 393248 | tf_op jit(solution)/shard_map/all_to_all | solution.py:233
  85.8 0.7 copy-done
  86.6 2.2 %shard_map.74 = bf16[32,2,16,128]{3,2,1,0:T(8,128)(2,1)} custom-call(s32[5]{0:T(128)} %stack.23.place_ref, bf16[32,3,16,128]{3,2,1,0:T(8,128)(2,1)} %copy-done), custom_call_target="tpu_custom_call" | custom-call | tf_op jit(solution)/shard_map/pallas_call | solution.py:174
  88.8 5.0 %all-to-all-start.2 = ((bf16[32,2,16,128]{3,2,1,0:T(8,128)(2,1)}), bf16[32,2,16,128]{3,2,1,0:T(8,128)(2,1)S(1)}, u32[]{:S(2)}, u32[]{:S(2)}) async-start(bf16[32,2,16,128]{3,2,1,0:T(8,128)(2,1)} %shard_map.74), calls=%async_computation.2 | async-start | bytes 524288 | tf_op jit(solution)/shard_map/all_to_all | solution.py:234
  93.8 10.4 %all-to-all-done.2.values_ref = bf16[32,2,16,128]{3,2,1,0:T(8,128)(2,1)S(1)} async-done(((bf16[32,2,16,128]{3,2,1,0:T(8,128)(2,1)}), bf16[32,2,16,128]{3,2,1,0:T(8,128)(2,1)S(1)}, u32[]{:S(2)}, u32[]{:S(2)}) %all-to-all-start.2) | async-done | bytes 262176 | tf_op jit(solution)/shard_map/all_to_all | solution.py:234
  104.2 0.7 copy-done.1
  104.9 2.4 %shard_map.75 = f32[8,32,64]{2,1,0:T(8,128)} custom-call(s32[5]{0:T(128)} %stack.23.place_ref, bf16[32,2,16,128]{3,2,1,0:T(8,128)(2,1)} %copy-done.1, bf16[128,2048]{1,0:T(8,128)(2,1)} %get-tuple-element.6.own_ref, bf16[128,2048]{1,0:T(8,128)(2,1)} %copy-done.3), custom_call_target="tpu_custom_call" | custom-call | tf_op jit(solution)/shard_map/pallas_call | solution.py:201
  107.3 1.0 reshape.13
  108.3 12.8 %all_to_all.28 = f32[8,1,2048]{2,1,0:T(1,128)S(1)} all-to-all(f32[8,1,2048]{2,1,0:T(1,128)S(1)} %reshape.13), channel_id=1, replica_groups=mesh['z'=8,'y'=4,'c'=2,'x'=4] {'c','x'}, dimensions={0} | all-to-all | bytes 131072 | tf_op jit(solution)/shard_map/all_to_all | solution.py:236
  121.1 0.5 broadcast.3
  121.7 0.8 reduce.1
  122.5 0.1 reshape.14
  122.6 0.6 fusion
  (28 shorter events, 0.1 us)
Async XLA Ops:
  0.0 48.1 %collective-permute-start.10 = (bf16[2,576,1024]{2,1,0:T(8,128)(2,1)}, bf16[2,576,1024]{2,1,0:T(8,128)(2,1)}, u32[]{:S(2)}, u32[]{:S(2)}) collective-permute-start(bf16[2,576,1024]{2,1,0:T(8,128)(2,1)} %bitcast.27), channel_id=1, source_target_pairs={{0,4},{4,0},{1,5},{5,1},{2,6},{6,2},{3,7},{7,3},{8,12},{12,8},{9,1... | collective-permute-start | bytes 7077896 | tf_op jit(solution)/shard_map/ppermute | solution.py:212
  3.2 44.9 %collective-permute-start.11 = (bf16[64,32,576]{2,1,0:T(8,128)(2,1)}, bf16[64,32,576]{2,1,0:T(8,128)(2,1)}, u32[]{:S(2)}, u32[]{:S(2)}) collective-permute-start(bf16[64,32,576]{2,1,0:T(8,128)(2,1)} %suf_own_ref.1), channel_id=1, source_target_pairs={{0,4},{4,0},{1,5},{5,1},{2,6},{6,2},{3,7},{7,3},{8,12},{12,8},{9,1... | collective-permute-start | bytes 7077896 | tf_op jit(solution)/shard_map/ppermute | solution.py:212
  11.3 6.7 %collective-permute-start = (bf16[2,16,576]{2,1,0:T(8,128)(2,1)S(1)}, bf16[2,16,576]{2,1,0:T(8,128)(2,1)S(1)}, u32[]{:S(2)}, u32[]{:S(2)}) collective-permute-start(bf16[2,16,576]{2,1,0:T(8,128)(2,1)S(1)} %bitcast.19), channel_id=1, source_target_pairs={{0,32},{32,64},{64,96},{96,128},{128,160},{160,192},{192,224},{224... | collective-permute-start | bytes 110600 | tf_op jit(solution)/shard_map/ppermute | solution.py:212
  11.4 9.2 %collective-permute-start.1 = (bf16[2,16,576]{2,1,0:T(8,128)(2,1)S(1)}, bf16[2,16,576]{2,1,0:T(8,128)(2,1)S(1)}, u32[]{:S(2)}, u32[]{:S(2)}) collective-permute-start(bf16[2,16,576]{2,1,0:T(8,128)(2,1)S(1)} %bitcast.20), channel_id=1, source_target_pairs={{0,64},{32,96},{64,128},{96,160},{128,192},{160,224},{192,0},{224,... | collective-permute-start | bytes 110600 | tf_op jit(solution)/shard_map/ppermute | solution.py:212
  14.3 8.9 %collective-permute-start.2 = (bf16[2,16,576]{2,1,0:T(8,128)(2,1)S(1)}, bf16[2,16,576]{2,1,0:T(8,128)(2,1)S(1)}, u32[]{:S(2)}, u32[]{:S(2)}) collective-permute-start(bf16[2,16,576]{2,1,0:T(8,128)(2,1)S(1)} %bitcast.21), channel_id=1, source_target_pairs={{0,96},{32,128},{64,160},{96,192},{128,224},{160,0},{192,32},{224,... | collective-permute-start | bytes 110600 | tf_op jit(solution)/shard_map/ppermute | solution.py:212
  18.1 7.6 %collective-permute-start.3 = (bf16[2,16,576]{2,1,0:T(8,128)(2,1)S(1)}, bf16[2,16,576]{2,1,0:T(8,128)(2,1)S(1)}, u32[]{:S(2)}, u32[]{:S(2)}) collective-permute-start(bf16[2,16,576]{2,1,0:T(8,128)(2,1)S(1)} %bitcast.23), channel_id=1, source_target_pairs={{0,128},{32,160},{64,192},{96,224},{128,0},{160,32},{192,64},{224,... | collective-permute-start | bytes 110600 | tf_op jit(solution)/shard_map/ppermute | solution.py:212
  20.6 6.3 %collective-permute-start.4 = (bf16[2,16,576]{2,1,0:T(8,128)(2,1)S(1)}, bf16[2,16,576]{2,1,0:T(8,128)(2,1)S(1)}, u32[]{:S(2)}, u32[]{:S(2)}) collective-permute-start(bf16[2,16,576]{2,1,0:T(8,128)(2,1)S(1)} %bitcast.24), channel_id=1, source_target_pairs={{0,160},{32,192},{64,224},{96,0},{128,32},{160,64},{192,96},{224,1... | collective-permute-start | bytes 110600 | tf_op jit(solution)/shard_map/ppermute | solution.py:212
  23.2 6.4 %collective-permute-start.5 = (bf16[2,16,576]{2,1,0:T(8,128)(2,1)S(1)}, bf16[2,16,576]{2,1,0:T(8,128)(2,1)S(1)}, u32[]{:S(2)}, u32[]{:S(2)}) collective-permute-start(bf16[2,16,576]{2,1,0:T(8,128)(2,1)S(1)} %bitcast.25), channel_id=1, source_target_pairs={{0,192},{32,224},{64,0},{96,32},{128,64},{160,96},{192,128},{224,1... | collective-permute-start | bytes 110600 | tf_op jit(solution)/shard_map/ppermute | solution.py:212
  25.6 4.8 %collective-permute-start.6 = (bf16[2,16,576]{2,1,0:T(8,128)(2,1)S(1)}, bf16[2,16,576]{2,1,0:T(8,128)(2,1)S(1)}, u32[]{:S(2)}, u32[]{:S(2)}) collective-permute-start(bf16[2,16,576]{2,1,0:T(8,128)(2,1)S(1)} %bitcast.26), channel_id=1, source_target_pairs={{0,224},{32,0},{64,32},{96,64},{128,96},{160,128},{192,160},{224,1... | collective-permute-start | bytes 110600 | tf_op jit(solution)/shard_map/ppermute | solution.py:212
  30.5 17.7 %copy-start.4 = (bf16[16,16,576]{2,1,0:T(8,128)(2,1)}, bf16[16,16,576]{2,1,0:T(8,128)(2,1)S(1)}, u32[]{:S(2)}) copy-start(bf16[16,16,576]{2,1,0:T(8,128)(2,1)S(1)} %constant_dynamic-update-slice_fusion.q0_ref) | copy-start | bytes 884740
  30.5 9.1 %collective-permute-start.7 = (bf16[16,16,576]{2,1,0:T(8,128)(2,1)S(1)}, bf16[16,16,576]{2,1,0:T(8,128)(2,1)S(1)}, u32[]{:S(2)}, u32[]{:S(2)}) collective-permute-start(bf16[16,16,576]{2,1,0:T(8,128)(2,1)S(1)} %constant_dynamic-update-slice_fusion.q0_ref), channel_id=1, source_target_pairs={{0,8},{8,16},{16,24},{24,0},{1,9},{9,17},{17,25},{25,1},{2,10},{10... | collective-permute-start | bytes 884744 | tf_op jit(solution)/shard_map/ppermute | solution.py:212
  31.9 15.9 %collective-permute-start.8 = (bf16[16,16,576]{2,1,0:T(8,128)(2,1)S(1)}, bf16[16,16,576]{2,1,0:T(8,128)(2,1)S(1)}, u32[]{:S(2)}, u32[]{:S(2)}) collective-permute-start(bf16[16,16,576]{2,1,0:T(8,128)(2,1)S(1)} %constant_dynamic-update-slice_fusion.q0_ref), channel_id=1, source_target_pairs={{0,16},{8,24},{16,0},{24,8},{1,17},{9,25},{17,1},{25,9},{2,18},{10... | collective-permute-start | bytes 884744 | tf_op jit(solution)/shard_map/ppermute | solution.py:212
  34.5 13.7 %collective-permute-start.9 = (bf16[16,16,576]{2,1,0:T(8,128)(2,1)S(1)}, bf16[16,16,576]{2,1,0:T(8,128)(2,1)S(1)}, u32[]{:S(2)}, u32[]{:S(2)}) collective-permute-start(bf16[16,16,576]{2,1,0:T(8,128)(2,1)S(1)} %constant_dynamic-update-slice_fusion.q0_ref), channel_id=1, source_target_pairs={{0,24},{8,0},{16,8},{24,16},{1,25},{9,1},{17,9},{25,17},{2,26},{10... | collective-permute-start | bytes 884744 | tf_op jit(solution)/shard_map/ppermute | solution.py:212
  39.3 32.8 %copy-start.2 = (bf16[4096,112]{0,1:T(8,128)(2,1)S(1)}, bf16[4096,112]{0,1:T(8,128)(2,1)}, u32[]{:S(2)}) copy-start(bf16[4096,112]{0,1:T(8,128)(2,1)} %param.13) | copy-start | bytes 2752516
  39.6 8.5 %copy-start.5 = (bf16[16,16,576]{2,1,0:T(8,128)(2,1)}, bf16[16,16,576]{2,1,0:T(8,128)(2,1)S(1)}, u32[]{:S(2)}) copy-start(bf16[16,16,576]{2,1,0:T(8,128)(2,1)S(1)} %collective-permute-done.7.q1_ref) | copy-start | bytes 884740
  47.8 0.8 copy-start.6
  48.1 0.7 copy-start.7
  65.3 20.5 %all-to-all-start.1 = ((bf16[32,3,16,128]{3,2,1,0:T(8,128)(2,1)}), bf16[32,3,16,128]{3,2,1,0:T(8,128)(2,1)S(1)}, u32[]{:S(2)}, u32[]{:S(2)}) async-start(bf16[32,3,16,128]{3,2,1,0:T(8,128)(2,1)} %shard_map.73), calls=%async_computation.1 | async-start | bytes 786432 | tf_op jit(solution)/shard_map/all_to_all | solution.py:233
  73.2 20.5 %collective-permute-start.12 = (bf16[128,2048]{1,0:T(8,128)(2,1)S(1)}, bf16[128,2048]{1,0:T(8,128)(2,1)S(1)}, u32[]{:S(2)}, u32[]{:S(2)}) collective-permute-start(bf16[128,2048]{1,0:T(8,128)(2,1)S(1)} %get-tuple-element.5), channel_id=1, source_target_pairs={{0,4},{4,0},{1,5},{5,1},{2,6},{6,2},{3,7},{7,3},{8,12},{12,8},{9,1... | collective-permute-start | bytes 1572872 | tf_op jit(solution)/shard_map/ppermute | solution.py:212
  85.8 0.7 copy-start
  88.8 15.4 %all-to-all-start.2 = ((bf16[32,2,16,128]{3,2,1,0:T(8,128)(2,1)}), bf16[32,2,16,128]{3,2,1,0:T(8,128)(2,1)S(1)}, u32[]{:S(2)}, u32[]{:S(2)}) async-start(bf16[32,2,16,128]{3,2,1,0:T(8,128)(2,1)} %shard_map.74), calls=%async_computation.2 | async-start | bytes 524288 | tf_op jit(solution)/shard_map/all_to_all | solution.py:234
  93.8 10.4 %copy-start.3 = (bf16[128,2048]{1,0:T(8,128)(2,1)}, bf16[128,2048]{1,0:T(8,128)(2,1)S(1)}, u32[]{:S(2)}) copy-start(bf16[128,2048]{1,0:T(8,128)(2,1)S(1)} %collective-permute-done.12.peer_ref) | copy-start | bytes 1572868
  104.2 0.7 copy-start.1

commit v2 on v0

v2 whole, which is shorter than its diff:
```python
import jax
import jax.numpy as jnp
from jax import lax
from jax.experimental import pallas as pl
from jax.experimental.pallas import tpu as pltpu
from jax.sharding import Mesh, PartitionSpec as P

ROPE = 64
NOPE = 128
SCALE = (NOPE + ROPE) ** (-0.5)
LOG2E = 1.4426950408889634
NZ, NY, NC, NX = 8, 4, 2, 4
CHIPS = NZ * NY
HEADS = 32
LAT = 512
VH = 128
COLUMNS = 28
MASKED = -1e30
TILE = 8
TILES = CHIPS // TILE + 1
SLOTS = TILES * TILE
KEYS = 64
PACKED = HEADS * (LAT + ROPE) // 128
MIB = 1024 * 1024

SMEM = pl.BlockSpec(memory_space=pltpu.SMEM)
BLOCK = pl.BlockSpec(memory_space=pltpu.VMEM)


def call(kernel, out, specs, out_specs, scratch, limit, flops, *args):
    return pl.pallas_call(
        kernel,
        out_shape=out,
        in_specs=specs,
        out_specs=out_specs,
        scratch_shapes=scratch,
        compiler_params=pltpu.CompilerParams(vmem_limit_bytes=limit * MIB),
        cost_estimate=pl.CostEstimate(flops=flops, bytes_accessed=4 * MIB, transcendentals=0),
    )(*args)


def nt_dot(a, b):
    return lax.dot_general(a, b, (((1,), (1,)), ((), ())), preferred_element_type=jnp.float32)


def pack_kernel(q_ref, out_ref):
    q = q_ref[0]
    parts = [q[:, c * 128:(c + 1) * 128] for c in range(LAT // 128)]
    rope = q[:, LAT:]
    parts.append(jnp.concatenate([rope[:HEADS // 2], rope[HEADS // 2:]], axis=1))
    packed = jnp.concatenate(parts, axis=0)
    for d in range(NZ):
        out_ref[d] = packed


def pack(queries):
    return call(
        pack_kernel,
        jax.ShapeDtypeStruct((NZ, PACKED, 128), jnp.bfloat16),
        [BLOCK],
        BLOCK,
        [],
        8,
        2**20,
        queries,
    )


IDS, LENS = 8, 8 + 2 * CHIPS


def prepare_kernel(
    facts_ref, own_in, uv_in, suf_own_ref, suf_peer_ref, table_ref, keys_ref, own_ref, uv_ref, sem
):
    copies = [
        pltpu.make_async_copy(own_in, own_ref, sem.at[0]),
        pltpu.make_async_copy(uv_in, uv_ref, sem.at[1]),
    ]
    for copy in copies:
        copy.start()
    core = facts_ref[2]
    first = jnp.int32(0)
    for t in range(CHIPS):
        first = first + jnp.where(facts_ref[IDS + 2 * t + core] != 0, 0, 1)
    edge = (first + TILE - 1) // TILE
    table_ref[CHIPS + SLOTS] = edge
    table_ref[CHIPS + SLOTS + 1] = edge + (CHIPS - first + TILE - 1) // TILE
    for s in range(SLOTS):
        table_ref[CHIPS + s] = 0
    low, high = jnp.int32(0), edge * TILE
    for t in range(CHIPS):
        second = facts_ref[IDS + 2 * t + core] != 0
        slot = jnp.where(second, high, low)
        low = low + jnp.where(second, 0, 1)
        high = high + jnp.where(second, 1, 0)
        table_ref[t] = slot
        table_ref[CHIPS + slot] = t
    for s in range(SLOTS):
        t = table_ref[CHIPS + s]
        keys_ref[s // 4, pl.ds(s % 4 * KEYS, 32), :] = suf_own_ref[2 * t + core]
        keys_ref[s // 4, pl.ds(s % 4 * KEYS + 32, 32), :] = suf_peer_ref[2 * t + core]
    for copy in copies:
        copy.wait()


def prepare(facts, own, uv, suf_own, suf_peer):
    away = pl.BlockSpec(memory_space=pl.ANY)
    return call(
        prepare_kernel,
        (
            jax.ShapeDtypeStruct((CHIPS + SLOTS + 8,), jnp.int32),
            jax.ShapeDtypeStruct((SLOTS // 4, 4 * KEYS, LAT + ROPE), jnp.bfloat16),
            jax.ShapeDtypeStruct(own.shape, own.dtype),
            jax.ShapeDtypeStruct(uv.shape, uv.dtype),
        ),
        [SMEM, away, away, BLOCK, BLOCK],
        (SMEM, BLOCK, BLOCK, BLOCK),
        [pltpu.SemaphoreType.DMA((2,))],
        20,
        2**28,
        facts, own, uv, suf_own, suf_peer,
    )


def attend_kernel(
    facts_ref, table_ref, q0_ref, q1_ref, q2_ref, q3_ref, own_ref, peer_ref, keys_ref, uv_ref, out_ref,
    q_ref, latent_ref, value_ref, stat_ref,
):
    own_base, peer_base, core, y = facts_ref[0], facts_ref[1], facts_ref[2], facts_ref[4]
    edge, used = table_ref[CHIPS + SLOTS], table_ref[CHIPS + SLOTS + 1]
    for j, ref in enumerate((q0_ref, q1_ref, q2_ref, q3_ref)):
        for z in range(NZ):
            q_ref[table_ref[z * NY + lax.rem(y + NY - j, NY)]] = ref[z]
    pairs = TILE * HEADS
    group = 4 * HEADS
    lane = lax.broadcasted_iota(jnp.int32, (group, 4 * KEYS), 1)
    part = lax.broadcasted_iota(jnp.int32, (group, 4 * KEYS), 0) // HEADS
    inside = lax.rem(lane, KEYS)
    position = jnp.where(inside < 32, own_base + inside, peer_base + inside - 32)
    position = jnp.where(lane // KEYS == part, position, 2**30)

    def query(slot):
        rope = q_ref[slot, LAT // 128 * HEADS:, :]
        parts = [q_ref[slot, c * HEADS:(c + 1) * HEADS, :] for c in range(LAT // 128)]
        parts.append(jnp.concatenate([rope[:, :ROPE], rope[:, ROPE:]], axis=0))
        return jnp.concatenate(parts, axis=1)

    def tile(i):
        k = jnp.where(i >= edge, 1, 0)
        q = jnp.concatenate([query(i * TILE + r) for r in range(TILE)], axis=0)
        s_own = jnp.dot(q, own_ref[k], preferred_element_type=jnp.float32)
        s_peer = jnp.dot(q, peer_ref[k], preferred_element_type=jnp.float32)
        suffix = []
        for g in range(2):
            limit = jnp.zeros((group, 4 * KEYS), jnp.int32)
            for r in range(4):
                t = table_ref[CHIPS + i * TILE + g * 4 + r]
                limit = jnp.where(part == r, facts_ref[LENS + 2 * t + core], limit)
            s = nt_dot(q[g * group:(g + 1) * group], keys_ref[i * 2 + g])
            suffix.append(jnp.where(position < limit, s, MASKED))
        s_suf = jnp.concatenate(suffix, axis=0)
        peak = jnp.maximum(
            jnp.maximum(s_own.max(-1, keepdims=True), s_peer.max(-1, keepdims=True)),
            s_suf.max(-1, keepdims=True),
        )
        w_own = jnp.exp2((s_own - peak) * (SCALE * LOG2E))
        w_peer = jnp.exp2((s_peer - peak) * (SCALE * LOG2E))
        w_suf = jnp.exp2((s_suf - peak) * (SCALE * LOG2E))
        total = (
            w_own.sum(-1, keepdims=True)
            + w_peer.sum(-1, keepdims=True)
            + w_suf.sum(-1, keepdims=True)
        )
        acc = nt_dot(w_own.astype(jnp.bfloat16), own_ref[k, :LAT, :])
        acc = acc + nt_dot(w_peer.astype(jnp.bfloat16), peer_ref[k, :LAT, :])
        w_suf = w_suf.astype(jnp.bfloat16)
        acc = acc + jnp.concatenate(
            [
                jnp.dot(
                    w_suf[g * group:(g + 1) * group],
                    keys_ref[i * 2 + g, :, :LAT],
                    preferred_element_type=jnp.float32,
                )
                for g in range(2)
            ],
            axis=0,
        )
        acc = acc / total
        for c in range(LAT // 128):
            latent_ref[c, pl.ds(i * pairs, pairs), :] = acc[:, c * 128:(c + 1) * 128]
        stat_ref[pl.ds(i * pairs, pairs), :] = jnp.broadcast_to(
            peak * SCALE + jnp.log(total), (pairs, 128)
        )

    for i in range(TILES - 1):
        tile(i)
    pl.when(used == TILES)(lambda: tile(TILES - 1))
    for h in range(0, HEADS, 2):
        rows = jnp.concatenate(
            [
                jnp.concatenate(
                    [latent_ref[c, pl.ds(h + d, SLOTS, stride=HEADS), :] for d in range(2)], axis=0
                )
                for c in range(LAT // 128)
            ],
            axis=1,
        ).astype(jnp.bfloat16)
        both = jnp.concatenate([uv_ref[h], uv_ref[h + 1]], axis=1)
        values = jnp.dot(rows, both, preferred_element_type=jnp.float32)
        value_ref[pl.ds(h, SLOTS, stride=HEADS), :] = values[:SLOTS, :VH]
        value_ref[pl.ds(h + 1, SLOTS, stride=HEADS), :] = values[SLOTS:, VH:]
    diagonal = lax.broadcasted_iota(jnp.int32, (128, 128), 0) == lax.broadcasted_iota(
        jnp.int32, (128, 128), 1
    )
    spots = [pl.multiple_of(table_ref[t] * HEADS, HEADS) for t in range(CHIPS)]
    for b in range(CHIPS // 4):
        picked = jnp.concatenate(
            [stat_ref[pl.ds(spots[b * 4 + i], HEADS), :] for i in range(4)], axis=0
        )
        mass = jnp.where(diagonal, picked, 0.0).sum(0, keepdims=True)
        high = mass.astype(jnp.bfloat16).astype(jnp.float32)
        middle = (mass - high).astype(jnp.bfloat16).astype(jnp.float32)
        stats = jnp.concatenate(
            [high, middle, mass - high - middle, jnp.zeros((5, 128), jnp.float32)], axis=0
        ).astype(jnp.bfloat16)
        for i in range(4):
            out_ref[b * 4 + i, pl.ds(HEADS, 8), :] = stats
    for t in range(CHIPS):
        out_ref[t, pl.ds(0, HEADS), :] = value_ref[pl.ds(spots[t], HEADS), :].astype(jnp.bfloat16)


def attend(facts, table, qs, own, peer, keys, uv):
    pairs = SLOTS * HEADS
    return call(
        attend_kernel,
        jax.ShapeDtypeStruct((CHIPS, HEADS + 8, VH), jnp.bfloat16),
        [SMEM] * 2 + [BLOCK] * 8,
        BLOCK,
        [
            pltpu.VMEM((SLOTS, PACKED, 128), jnp.bfloat16),
            pltpu.VMEM((LAT // 128, pairs, 128), jnp.float32),
            pltpu.VMEM((pairs, VH), jnp.float32),
            pltpu.VMEM((pairs, 128), jnp.float32),
        ],
        30,
        2 * pairs * 2200 * 1088,
        facts, table, *qs, own, peer, keys, uv,
    )


def combine_kernel(facts_ref, got_ref, out_ref, turned_ref):
    start = pl.multiple_of(lax.rem(facts_ref[3], 4) * HEADS, HEADS)
    stats = got_ref[:, HEADS:HEADS + 8, :].astype(jnp.float32)
    mass = stats[:, 0] + stats[:, 1] + stats[:, 2]
    weight = jnp.exp(mass - mass.max(0, keepdims=True))
    weight = weight / weight.sum(0, keepdims=True)
    turned_ref[...] = jnp.concatenate([weight, jnp.zeros((96, 128), jnp.float32)], axis=0).T
    column = turned_ref[pl.ds(start, HEADS), :]
    total = jnp.zeros((HEADS, VH), jnp.float32)
    for d in range(CHIPS):
        total = total + column[:, d:d + 1] * got_ref[d, :HEADS, :].astype(jnp.float32)
    total = total.astype(jnp.bfloat16)
    for d in range(CHIPS):
        out_ref[d] = total


def combine(facts, got):
    return call(
        combine_kernel,
        jax.ShapeDtypeStruct((CHIPS, HEADS, VH), jnp.bfloat16),
        [SMEM, BLOCK],
        BLOCK,
        [pltpu.VMEM((128, 128), jnp.float32)],
        4,
        2**24,
        facts, got,
    )


def project_kernel(facts_ref, values_ref, own_ref, peer_ref, out_ref, wide_ref):
    core = facts_ref[2]
    for t in range(CHIPS):
        wide_ref[pl.ds(t * HEADS, HEADS), :] = values_ref[t].astype(jnp.float32)
    flat = jnp.concatenate(
        [wide_ref[pl.ds(h, CHIPS, stride=HEADS), :].astype(jnp.bfloat16) for h in range(HEADS)],
        axis=1,
    )
    for ref, to in ((own_ref, core), (peer_ref, 1 - core)):
        shares = nt_dot(ref[...], flat)
        for x in range(NX):
            block = jnp.concatenate(
                [shares[x * COLUMNS:(x + 1) * COLUMNS], jnp.zeros((4, CHIPS), jnp.float32)], axis=0
            )
            out_ref[to * NX + x] = jnp.concatenate(
                [block[8 * i:8 * i + 8] for i in range(4)], axis=1
            )


def project(facts, values, own, peer):
    return call(
        project_kernel,
        jax.ShapeDtypeStruct((NC * NX, 8, 128), jnp.float32),
        [SMEM, BLOCK, BLOCK, BLOCK],
        BLOCK,
        [pltpu.VMEM((CHIPS * HEADS, VH), jnp.float32)],
        8,
        2**27,
        facts, values, own, peer,
    )


def finish_kernel(got_ref, out_ref):
    sides = []
    for core in range(NC):
        summed = sum(got_ref[core * NX + x] for x in range(1, NX)) + got_ref[core * NX]
        sides.append(jnp.concatenate([summed[:, 32 * i:32 * i + 32] for i in range(4)], axis=0))
    both = jnp.concatenate(sides, axis=1).astype(jnp.bfloat16)
    lane = lax.broadcasted_iota(jnp.int32, (64, 64), 0)
    row = lax.broadcasted_iota(jnp.int32, (64, 64), 1)
    chosen = (lane == lax.rem(row, 2) * 32 + row // 2).astype(jnp.float32).astype(jnp.bfloat16)
    mixed = jnp.dot(both, chosen, preferred_element_type=jnp.float32).astype(jnp.bfloat16)
    out_ref[...] = mixed[:COLUMNS]


def finish(got):
    return call(
        finish_kernel,
        jax.ShapeDtypeStruct((COLUMNS, 64), jnp.bfloat16),
        [BLOCK],
        BLOCK,
        [],
        4,
        2**20,
        got,
    )


def swap(x):
    return lax.ppermute(x, "c", [(0, 1), (1, 0)])


def per_device(queries, prompt_cache, suffix_cache, prompt_ids, suffix_len, w_uv, w_out):
    core = lax.axis_index("c")
    chip = lax.axis_index("z") * NY + lax.axis_index("y")
    zero = jnp.zeros((), jnp.int32)
    place = [(chip * 2 + core) * 32, (chip * 2 + 1 - core) * 32, core, chip, lax.axis_index("y")]
    facts = jnp.concatenate([jnp.stack(place + [zero] * 3), prompt_ids, suffix_len])
    facts, queries = lax.optimization_barrier((facts, queries))
    own = jnp.transpose(prompt_cache, (0, 2, 1))
    peer, suf_peer = swap(own), swap(suffix_cache)
    along_z = lax.all_to_all(pack(queries), "z", 0, 0, tiled=True)
    along_z, suf_peer = lax.optimization_barrier((along_z, suf_peer))
    qs = [along_z] + [
        lax.ppermute(along_z, "y", [(i, (i + j) % NY) for i in range(NY)]) for j in range(1, NY)
    ]
    table, keys, own, uv = prepare(facts, own, w_uv, suffix_cache, suf_peer)
    parts = attend(facts, table, qs, own, peer, keys, uv)
    parts, w_t = lax.optimization_barrier((parts, w_out.T))
    w_peer = swap(w_t)
    got = lax.all_to_all(parts, ("z", "y"), 0, 0, tiled=True)
    values = lax.all_to_all(combine(facts, got), ("z", "y"), 0, 0, tiled=True)
    shares = project(facts, values, w_t, w_peer)
    return finish(lax.all_to_all(shares, ("c", "x"), 0, 0, tiled=True)).T


def solution(mesh):
    whole = ("z", "y", "c", "x")
    kv = ("z", "y", "c")
    split = Mesh(mesh.devices.reshape(NZ, NY, NC, NX), whole)
    placed = (
        P(kv, "x", None),
        P(None, kv, None),
        P(None, kv, None),
        P(),
        P(),
        P("x", None, None),
        P("x", kv),
    )
    return jax.shard_map(
        per_device, mesh=split, in_specs=placed, out_specs=P(None, whole), check_vma=False
    )
```

time: 930 us -> 104 us (0.11)
  blocking collectives: 755 us -> 30.3 us
  waiting for transfers between devices: 84.1 us -> 23.6 us
  matrix products: 40.5 us -> 0 us
  Pallas kernels: 0 us -> 21 us
  starting transfers between devices: 2.67 us -> 21.9 us
  between operations: 14.2 us -> 0.08 us
  other arithmetic: 11.2 us -> 0 us
    psum x2 -> x0, blocking collectives: 502 us -> none  [the longest x1 255 us: per_device(): head_values = lax.psum(value_part, 'kv').astype(jnp.bfloat16)]
    pmax x1 -> x0, blocking collectives: 243 us -> none  [global_top(): return lax.pmax(peak_here, 'kv')]
    all_gather x1 -> x0, waiting for transfers between devices: 83.4 us -> none  [per_device(): gathered = lax.all_gather(queries, 'kv', axis=0, tiled=True)]
    dot_general x8 -> x0, matrix products: 40.5 us -> none  [the longest x2 14.5 us: per_device(): jnp.einsum('rhe,te->rht', gathered, prompt_cache[k], preferred_element_ty...]
    all_to_all x0 -> x2, blocking collectives: none -> 30.3 us  [the longest x1 17.5 us: per_device(): along_z = lax.all_to_all(pack(queries), 'z', 0, 0, tiled=True)]
    all_to_all x0 -> x2, waiting for transfers between devices: none -> 21.1 us  [the longest x1 10.7 us: per_device(): got = lax.all_to_all(parts, ('z', 'y'), 0, 0, tiled=True)]
    pallas_call x0 -> x6, Pallas kernels: none -> 21 us  [call(): pl.pallas_call(kernel, out_shape=out, in_specs=specs, out_specs=out_specs...]
    all_to_all x0 -> x2, starting transfers between devices: none -> 12.3 us  [the longest x1 7.15 us: per_device(): got = lax.all_to_all(parts, ('z', 'y'), 0, 0, tiled=True)]
  transfers between devices with their start and end apart: 3 -> 8, of which waited for: 1 -> 4; matrix products, arithmetic and copies ran while one was open for 1% -> 1% of each run, Pallas kernels for 0% -> 4%
where the time goes in v2:
time: 104 us
  blocking collectives  30.3 us (29%)
  waiting for transfers between devices  23.6 us (23%)
  starting transfers between devices  21.9 us (21%)
  Pallas kernels  21 us (20%)
  local copies, waits for them, and re-layouts  7.13 us (7%)
    pallas_call x6, Pallas kernels, call(): pl.pallas_call(kernel, out_shape=out, in_specs=specs, out_specs=out_specs...  21 us
    all_to_all x1, blocking collectives, per_device(): along_z = lax.all_to_all(pack(queries), 'z', 0, 0, tiled=True)  17.5 us
    all_to_all x1, blocking collectives, per_device(): return finish(lax.all_to_all(shares, ('c', 'x'), 0, 0, tiled=True)).T  12.8 us
    all_to_all x1, waiting for transfers between devices, per_device(): got = lax.all_to_all(parts, ('z', 'y'), 0, 0, tiled=True)  10.7 us
    all_to_all x1, waiting for transfers between devices, per_device(): values = lax.all_to_all(combine(facts, got), ('z', 'y'), 0, 0, tiled=True)  10.4 us
    all_to_all x1, starting transfers between devices, per_device(): got = lax.all_to_all(parts, ('z', 'y'), 0, 0, tiled=True)  7.15 us
    unnamed x10, local copies, waits for them, and re-layouts  6.38 us
    all_to_all x1, starting transfers between devices, per_device(): values = lax.all_to_all(combine(facts, got), ('z', 'y'), 0, 0, tiled=True)  5.15 us
  transfers between devices with their start and end apart: 8, of which 4 were waited for; matrix products, arithmetic and copies ran while one was open for 1% of the time, Pallas kernels for 4%

profile of v2, /device:TPU:1, one launch (start us, length us, event | category | flops | bytes accessed | tf_op | source)
XLA Modules:
  0.0 104.0 jit_solution(10409990649730064434)
XLA Ops:
  0.0 3.2 %collective-permute-start = (bf16[64,32,576]{2,1,0:T(8,128)(2,1)}, bf16[64,32,576]{2,1,0:T(8,128)(2,1)S(1)}, u32[]{:S(2)}, u32[]{:S(2)}) collective-permute-start(bf16[64,32,576]{2,1,0:T(8,128)(2,1)} %suf_own_ref.1), channel_id=1, source_target_pairs={{0,4},{4,0},{1,5},{5,1},{2,6},{6,2},{3,7},{7,3},{8,12},{12,8},{9,1... | collective-permute-start | bytes 7077896 | tf_op jit(solution)/shard_map/ppermute | solution.py:339
  3.2 0.0 collective-permute-start.4
  3.2 0.8 concatenate.3.facts_ref
  4.0 0.0 copy-start.4
  4.0 0.8 copy-done.4
  4.8 0.1 shard_map.73
  4.9 17.5 %all_to_all.20.q0_ref = bf16[8,144,128]{2,1,0:T(8,128)(2,1)S(1)} all-to-all(bf16[8,144,128]{2,1,0:T(8,128)(2,1)S(1)} %shard_map.73), channel_id=1, replica_groups=mesh['z'=8,'y'=4,'c'=2,'x'=4] {'z'}, dimensions={0} | all-to-all | bytes 589824 | tf_op jit(solution)/shard_map/all_to_all | solution.py:351
  22.4 0.0 collective-permute-done.suf_peer_ref
  22.4 1.3 %collective-permute-start.1 = (bf16[8,144,128]{2,1,0:T(8,128)(2,1)S(1)}, bf16[8,144,128]{2,1,0:T(8,128)(2,1)S(1)}, u32[]{:S(2)}, u32[]{:S(2)}) collective-permute-start(bf16[8,144,128]{2,1,0:T(8,128)(2,1)S(1)} %all_to_all.20.q0_ref), channel_id=1, source_target_pairs={{0,8},{8,16},{16,24},{24,0},{1,9},{9,17},{17,25},{25,1},{2,10},{10... | collective-permute-start | bytes 884744 | tf_op jit(solution)/shard_map/ppermute | solution.py:354
  23.7 2.6 %collective-permute-start.2 = (bf16[8,144,128]{2,1,0:T(8,128)(2,1)S(1)}, bf16[8,144,128]{2,1,0:T(8,128)(2,1)S(1)}, u32[]{:S(2)}, u32[]{:S(2)}) collective-permute-start(bf16[8,144,128]{2,1,0:T(8,128)(2,1)S(1)} %all_to_all.20.q0_ref), channel_id=1, source_target_pairs={{0,16},{8,24},{16,0},{24,8},{1,17},{9,25},{17,1},{25,9},{2,18},{10... | collective-permute-start | bytes 884744 | tf_op jit(solution)/shard_map/ppermute | solution.py:354
  26.3 1.1 %collective-permute-start.3 = (bf16[8,144,128]{2,1,0:T(8,128)(2,1)S(1)}, bf16[8,144,128]{2,1,0:T(8,128)(2,1)S(1)}, u32[]{:S(2)}, u32[]{:S(2)}) collective-permute-start(bf16[8,144,128]{2,1,0:T(8,128)(2,1)S(1)} %all_to_all.20.q0_ref), channel_id=1, source_target_pairs={{0,24},{8,0},{16,8},{24,16},{1,25},{9,1},{17,9},{25,17},{2,26},{10... | collective-permute-start | bytes 884744 | tf_op jit(solution)/shard_map/ppermute | solution.py:354
  27.4 0.0 copy-start
  27.4 2.2 %copy-done = bf16[32,512,128]{2,1,0:T(8,128)(2,1)S(1)} copy-done((bf16[32,512,128]{2,1,0:T(8,128)(2,1)S(1)}, bf16[32,512,128]{2,1,0:T(8,128)(2,1)}, u32[]{:S(2)}) %copy-start) | copy-done | bytes 4194328
  29.6 0.0 copy-start.1
  29.6 1.7 %copy-done.1 = bf16[64,32,576]{2,1,0:T(8,128)(2,1)S(1)} copy-done((bf16[64,32,576]{2,1,0:T(8,128)(2,1)S(1)}, bf16[64,32,576]{2,1,0:T(8,128)(2,1)}, u32[]{:S(2)}) %copy-start.1) | copy-done | bytes 2359320
  31.3 0.0 copy-start.2
  31.3 1.7 %copy-done.2 = bf16[2,1024,576]{1,2,0:T(8,128)(2,1)S(1)} copy-done((bf16[2,1024,576]{1,2,0:T(8,128)(2,1)S(1)}, bf16[2,1024,576]{1,2,0:T(8,128)(2,1)}, u32[]{:S(2)}) %copy-start.2) | copy-done | bytes 2359320
  33.0 2.1 %shard_map.74 = (s32[80]{0:T(128)S(1)}, bf16[10,256,576]{2,1,0:T(8,128)(2,1)S(1)}, bf16[2,576,1024]{2,1,0:T(8,128)(2,1)S(1)}, bf16[32,512,128]{2,1,0:T(8,128)(2,1)S(1)}) custom-call(s32[136]{0:T(256)S(1)} %concatenate.3.facts_ref, bf16[2,576,1024]{2,1,0:T(8,128)(2,1)S(1)} %bitcast.9, bf16[32,512,128]{2,1,0:T(8,128)(2,1)S(1)} %copy-done, ...), custom_call_target="tpu_custom_call" | custom-call | flops 268435456 | bytes 4194304 | tf_op jit(solution)/shard_map/pallas_call | solution.py:31
  35.1 0.0 collective-permute-done.4.peer_ref
  35.1 0.0 collective-permute-done.1.q1_ref
  35.1 2.3 %collective-permute-done.2.q2_ref = bf16[8,144,128]{2,1,0:T(8,128)(2,1)S(1)} collective-permute-done((bf16[8,144,128]{2,1,0:T(8,128)(2,1)S(1)}, bf16[8,144,128]{2,1,0:T(8,128)(2,1)S(1)}, u32[]{:S(2)}, u32[]{:S(2)}) %collective-permute-start.2) | collective-permute-done | bytes 294944 | tf_op jit(solution)/shard_map/ppermute | solution.py:354
  37.4 0.1 collective-permute-done.3.q3_ref
  37.6 0.0 copy-start.3
  37.6 15.0 %shard_map.75 = bf16[32,40,128]{2,1,0:T(8,128)(2,1)} custom-call(s32[136]{0:T(256)S(1)} %concatenate.3.facts_ref, s32[80]{0:T(128)S(1)} %get-tuple-element.18.table_ref, bf16[8,144,128]{2,1,0:T(8,128)(2,1)S(1)} %all_to_all.20.q0_ref, bf16[8,144,128]{2,1,0:T(8,128)(2,1)S(1)} %collective-permute-done.1.q1_ref, ...), custom_call_target="tpu_custom_call" | custom-call | flops 6127616000 | bytes 4194304 | tf_op jit(solution)/shard_map/pallas_call | solution.py:31
  52.5 7.2 %all-to-all-start.1 = ((bf16[32,40,128]{2,1,0:T(8,128)(2,1)}), bf16[32,40,128]{2,1,0:T(8,128)(2,1)S(1)}, u32[]{:S(2)}, u32[]{:S(2)}) async-start(bf16[32,40,128]{2,1,0:T(8,128)(2,1)} %shard_map.75), calls=%async_computation.1 | async-start | bytes 655360 | tf_op jit(solution)/shard_map/all_to_all | solution.py:360
  59.7 0.0 copy-done.3
  59.7 1.4 %collective-permute-start.5 = (bf16[112,4096]{1,0:T(8,128)(2,1)S(1)}, bf16[112,4096]{1,0:T(8,128)(2,1)S(1)}, u32[]{:S(2)}, u32[]{:S(2)}) collective-permute-start(bf16[112,4096]{1,0:T(8,128)(2,1)S(1)} %bitcast.10), channel_id=1, source_target_pairs={{0,4},{4,0},{1,5},{5,1},{2,6},{6,2},{3,7},{7,3},{8,12},{12,8},{9,1... | collective-permute-start | bytes 2752520 | tf_op jit(solution)/shard_map/ppermute | solution.py:339
  61.1 10.7 %all-to-all-done.1.got_ref = bf16[32,40,128]{2,1,0:T(8,128)(2,1)S(1)} async-done(((bf16[32,40,128]{2,1,0:T(8,128)(2,1)}), bf16[32,40,128]{2,1,0:T(8,128)(2,1)S(1)}, u32[]{:S(2)}, u32[]{:S(2)}) %all-to-all-start.1) | async-done | bytes 327712 | tf_op jit(solution)/shard_map/all_to_all | solution.py:360
  71.8 1.7 %shard_map.76 = bf16[32,32,128]{2,1,0:T(8,128)(2,1)} custom-call(s32[136]{0:T(256)S(1)} %concatenate.3.facts_ref, bf16[32,40,128]{2,1,0:T(8,128)(2,1)S(1)} %all-to-all-done.1.got_ref), custom_call_target="tpu_custom_call" | custom-call | flops 16777216 | bytes 4194304 | tf_op jit(solution)/shard_map/pallas_call | solution.py:31
  73.5 5.2 %all-to-all-start.2 = ((bf16[32,32,128]{2,1,0:T(8,128)(2,1)}), bf16[32,32,128]{2,1,0:T(8,128)(2,1)S(1)}, u32[]{:S(2)}, u32[]{:S(2)}) async-start(bf16[32,32,128]{2,1,0:T(8,128)(2,1)} %shard_map.76), calls=%async_computation.2 | async-start | bytes 524288 | tf_op jit(solution)/shard_map/all_to_all | solution.py:361
  78.7 0.0 collective-permute-done.5.peer_ref
  78.7 10.4 %all-to-all-done.2.values_ref = bf16[32,32,128]{2,1,0:T(8,128)(2,1)S(1)} async-done(((bf16[32,32,128]{2,1,0:T(8,128)(2,1)}), bf16[32,32,128]{2,1,0:T(8,128)(2,1)S(1)}, u32[]{:S(2)}, u32[]{:S(2)}) %all-to-all-start.2) | async-done | bytes 262176 | tf_op jit(solution)/shard_map/all_to_all | solution.py:361
  89.1 1.3 %shard_map.77 = f32[8,8,128]{2,1,0:T(8,128)S(1)} custom-call(s32[136]{0:T(256)S(1)} %concatenate.3.facts_ref, bf16[32,32,128]{2,1,0:T(8,128)(2,1)S(1)} %all-to-all-done.2.values_ref, bf16[112,4096]{1,0:T(8,128)(2,1)S(1)} %bitcast.11, bf16[112,4096]{1,0:T(8,128)(2,1)S(1)} %collective-permute-done.5.peer_ref), custom_call_target="tpu_custom_call" | custom-call | flops 134217728 | bytes 4194304 | tf_op jit(solution)/shard_map/pallas_call | solution.py:31
  90.3 12.8 %all_to_all.21.got_ref = f32[8,8,128]{2,1,0:T(8,128)S(1)} all-to-all(f32[8,8,128]{2,1,0:T(8,128)S(1)} %shard_map.77), channel_id=1, replica_groups=mesh['z'=8,'y'=4,'c'=2,'x'=4] {'c','x'}, dimensions={0} | all-to-all | bytes 65536 | tf_op jit(solution)/shard_map/all_to_all | solution.py:363
  103.1 0.9 shard_map.78
  (1 shorter events, 0.0 us)
Async XLA Ops:
  0.0 22.4 %collective-permute-start = (bf16[64,32,576]{2,1,0:T(8,128)(2,1)}, bf16[64,32,576]{2,1,0:T(8,128)(2,1)S(1)}, u32[]{:S(2)}, u32[]{:S(2)}) collective-permute-start(bf16[64,32,576]{2,1,0:T(8,128)(2,1)} %suf_own_ref.1), channel_id=1, source_target_pairs={{0,4},{4,0},{1,5},{5,1},{2,6},{6,2},{3,7},{7,3},{8,12},{12,8},{9,1... | collective-permute-start | bytes 7077896 | tf_op jit(solution)/shard_map/ppermute | solution.py:339
  3.2 31.8 %collective-permute-start.4 = (bf16[2,576,1024]{2,1,0:T(8,128)(2,1)}, bf16[2,576,1024]{2,1,0:T(8,128)(2,1)}, u32[]{:S(2)}, u32[]{:S(2)}) collective-permute-start(bf16[2,576,1024]{2,1,0:T(8,128)(2,1)} %bitcast.8), channel_id=1, source_target_pairs={{0,4},{4,0},{1,5},{5,1},{2,6},{6,2},{3,7},{7,3},{8,12},{12,8},{9,1... | collective-permute-start | bytes 7077896 | tf_op jit(solution)/shard_map/ppermute | solution.py:339
  4.0 0.8 copy-start.4
  22.4 12.7 %collective-permute-start.1 = (bf16[8,144,128]{2,1,0:T(8,128)(2,1)S(1)}, bf16[8,144,128]{2,1,0:T(8,128)(2,1)S(1)}, u32[]{:S(2)}, u32[]{:S(2)}) collective-permute-start(bf16[8,144,128]{2,1,0:T(8,128)(2,1)S(1)} %all_to_all.20.q0_ref), channel_id=1, source_target_pairs={{0,8},{8,16},{16,24},{24,0},{1,9},{9,17},{17,25},{25,1},{2,10},{10... | collective-permute-start | bytes 884744 | tf_op jit(solution)/shard_map/ppermute | solution.py:354
  23.7 13.7 %collective-permute-start.2 = (bf16[8,144,128]{2,1,0:T(8,128)(2,1)S(1)}, bf16[8,144,128]{2,1,0:T(8,128)(2,1)S(1)}, u32[]{:S(2)}, u32[]{:S(2)}) collective-permute-start(bf16[8,144,128]{2,1,0:T(8,128)(2,1)S(1)} %all_to_all.20.q0_ref), channel_id=1, source_target_pairs={{0,16},{8,24},{16,0},{24,8},{1,17},{9,25},{17,1},{25,9},{2,18},{10... | collective-permute-start | bytes 884744 | tf_op jit(solution)/shard_map/ppermute | solution.py:354
  26.3 11.3 %collective-permute-start.3 = (bf16[8,144,128]{2,1,0:T(8,128)(2,1)S(1)}, bf16[8,144,128]{2,1,0:T(8,128)(2,1)S(1)}, u32[]{:S(2)}, u32[]{:S(2)}) collective-permute-start(bf16[8,144,128]{2,1,0:T(8,128)(2,1)S(1)} %all_to_all.20.q0_ref), channel_id=1, source_target_pairs={{0,24},{8,0},{16,8},{24,16},{1,25},{9,1},{17,9},{25,17},{2,26},{10... | collective-permute-start | bytes 884744 | tf_op jit(solution)/shard_map/ppermute | solution.py:354
  27.4 2.2 %copy-start = (bf16[32,512,128]{2,1,0:T(8,128)(2,1)S(1)}, bf16[32,512,128]{2,1,0:T(8,128)(2,1)}, u32[]{:S(2)}) copy-start(bf16[32,512,128]{2,1,0:T(8,128)(2,1)} %uv_in.1) | copy-start | bytes 12582916
  29.6 1.7 %copy-start.1 = (bf16[64,32,576]{2,1,0:T(8,128)(2,1)S(1)}, bf16[64,32,576]{2,1,0:T(8,128)(2,1)}, u32[]{:S(2)}) copy-start(bf16[64,32,576]{2,1,0:T(8,128)(2,1)} %suf_own_ref.1) | copy-start | bytes 7077892
  31.3 1.7 %copy-start.2 = (bf16[2,1024,576]{1,2,0:T(8,128)(2,1)S(1)}, bf16[2,1024,576]{1,2,0:T(8,128)(2,1)}, u32[]{:S(2)}) copy-start(bf16[2,1024,576]{1,2,0:T(8,128)(2,1)} %param.8) | copy-start | bytes 7077892
  37.6 22.1 %copy-start.3 = (bf16[4096,112]{0,1:T(8,128)(2,1)S(1)}, bf16[4096,112]{0,1:T(8,128)(2,1)}, u32[]{:S(2)}) copy-start(bf16[4096,112]{0,1:T(8,128)(2,1)} %param.13) | copy-start | bytes 2752516
  52.5 19.3 %all-to-all-start.1 = ((bf16[32,40,128]{2,1,0:T(8,128)(2,1)}), bf16[32,40,128]{2,1,0:T(8,128)(2,1)S(1)}, u32[]{:S(2)}, u32[]{:S(2)}) async-start(bf16[32,40,128]{2,1,0:T(8,128)(2,1)} %shard_map.75), calls=%async_computation.1 | async-start | bytes 655360 | tf_op jit(solution)/shard_map/all_to_all | solution.py:360
  59.7 19.0 %collective-permute-start.5 = (bf16[112,4096]{1,0:T(8,128)(2,1)S(1)}, bf16[112,4096]{1,0:T(8,128)(2,1)S(1)}, u32[]{:S(2)}, u32[]{:S(2)}) collective-permute-start(bf16[112,4096]{1,0:T(8,128)(2,1)S(1)} %bitcast.10), channel_id=1, source_target_pairs={{0,4},{4,0},{1,5},{5,1},{2,6},{6,2},{3,7},{7,3},{8,12},{12,8},{9,1... | collective-permute-start | bytes 2752520 | tf_op jit(solution)/shard_map/ppermute | solution.py:339
  73.5 15.6 %all-to-all-start.2 = ((bf16[32,32,128]{2,1,0:T(8,128)(2,1)}), bf16[32,32,128]{2,1,0:T(8,128)(2,1)S(1)}, u32[]{:S(2)}, u32[]{:S(2)}) async-start(bf16[32,32,128]{2,1,0:T(8,128)(2,1)} %shard_map.76), calls=%async_computation.2 | async-start | bytes 524288 | tf_op jit(solution)/shard_map/all_to_all | solution.py:361

commit v3 on v2

--- a/solution.py
+++ b/solution.py
@@ -17,8 +17,9 @@
 COLUMNS = 28
 MASKED = -1e30
 TILE = 8
-TILES = CHIPS // TILE + 1
-SLOTS = TILES * TILE
+SPARE = TILE // 2
+USED = CHIPS + SPARE
+SLOTS = 40
 KEYS = 64
 PACKED = HEADS * (LAT + ROPE) // 128
 MIB = 1024 * 1024
@@ -82,20 +83,27 @@
     first = jnp.int32(0)
     for t in range(CHIPS):
         first = first + jnp.where(facts_ref[IDS + 2 * t + core] != 0, 0, 1)
-    edge = (first + TILE - 1) // TILE
-    table_ref[CHIPS + SLOTS] = edge
-    table_ref[CHIPS + SLOTS + 1] = edge + (CHIPS - first + TILE - 1) // TILE
+    table_ref[CHIPS + SLOTS] = first
+    border = first // TILE * TILE
+    few = first - border <= SPARE
     for s in range(SLOTS):
         table_ref[CHIPS + s] = 0
-    low, high = jnp.int32(0), edge * TILE
+    low, high = jnp.int32(0), first
     for t in range(CHIPS):
         second = facts_ref[IDS + 2 * t + core] != 0
         slot = jnp.where(second, high, low)
+        moved = jnp.where(
+            second,
+            jnp.logical_and(jnp.logical_not(few), slot < border + TILE),
+            jnp.logical_and(few, slot >= border),
+        )
+        base = jnp.where(second, first, border)
+        slot = jnp.where(moved, CHIPS + slot - base, slot)
         low = low + jnp.where(second, 0, 1)
         high = high + jnp.where(second, 1, 0)
         table_ref[t] = slot
         table_ref[CHIPS + slot] = t
-    for s in range(SLOTS):
+    for s in range(USED):
         t = table_ref[CHIPS + s]
         keys_ref[s // 4, pl.ds(s % 4 * KEYS, 32), :] = suf_own_ref[2 * t + core]
         keys_ref[s // 4, pl.ds(s % 4 * KEYS + 32, 32), :] = suf_peer_ref[2 * t + core]
@@ -109,7 +117,7 @@
         prepare_kernel,
         (
             jax.ShapeDtypeStruct((CHIPS + SLOTS + 8,), jnp.int32),
-            jax.ShapeDtypeStruct((SLOTS // 4, 4 * KEYS, LAT + ROPE), jnp.bfloat16),
+            jax.ShapeDtypeStruct((USED // 4, 4 * KEYS, LAT + ROPE), jnp.bfloat16),
             jax.ShapeDtypeStruct(own.shape, own.dtype),
             jax.ShapeDtypeStruct(uv.shape, uv.dtype),
         ),
@@ -127,11 +135,10 @@
     q_ref, latent_ref, value_ref, stat_ref,
 ):
     own_base, peer_base, core, y = facts_ref[0], facts_ref[1], facts_ref[2], facts_ref[4]
-    edge, used = table_ref[CHIPS + SLOTS], table_ref[CHIPS + SLOTS + 1]
+    first = table_ref[CHIPS + SLOTS]
     for j, ref in enumerate((q0_ref, q1_ref, q2_ref, q3_ref)):
         for z in range(NZ):
             q_ref[table_ref[z * NY + lax.rem(y + NY - j, NY)]] = ref[z]
-    pairs = TILE * HEADS
     group = 4 * HEADS
     lane = lax.broadcasted_iota(jnp.int32, (group, 4 * KEYS), 1)
     part = lax.broadcasted_iota(jnp.int32, (group, 4 * KEYS), 0) // HEADS
@@ -145,18 +152,20 @@
         parts.append(jnp.concatenate([rope[:, :ROPE], rope[:, ROPE:]], axis=0))
         return jnp.concatenate(parts, axis=1)
 
-    def tile(i):
-        k = jnp.where(i >= edge, 1, 0)
-        q = jnp.concatenate([query(i * TILE + r) for r in range(TILE)], axis=0)
+    def tile(start, count, k):
+        pairs = count * HEADS
+        here = pl.ds(start * HEADS, pairs)
+        groups = range(start // 4, (start + count) // 4)
+        q = jnp.concatenate([query(start + r) for r in range(count)], axis=0)
         s_own = jnp.dot(q, own_ref[k], preferred_element_type=jnp.float32)
         s_peer = jnp.dot(q, peer_ref[k], preferred_element_type=jnp.float32)
         suffix = []
-        for g in range(2):
+        for g, n in enumerate(groups):
             limit = jnp.zeros((group, 4 * KEYS), jnp.int32)
             for r in range(4):
-                t = table_ref[CHIPS + i * TILE + g * 4 + r]
+                t = table_ref[CHIPS + n * 4 + r]
                 limit = jnp.where(part == r, facts_ref[LENS + 2 * t + core], limit)
-            s = nt_dot(q[g * group:(g + 1) * group], keys_ref[i * 2 + g])
+            s = nt_dot(q[g * group:(g + 1) * group], keys_ref[n])
             suffix.append(jnp.where(position < limit, s, MASKED))
         s_suf = jnp.concatenate(suffix, axis=0)
         peak = jnp.maximum(
@@ -178,23 +187,24 @@
             [
                 jnp.dot(
                     w_suf[g * group:(g + 1) * group],
-                    keys_ref[i * 2 + g, :, :LAT],
+                    keys_ref[n, :, :LAT],
                     preferred_element_type=jnp.float32,
                 )
-                for g in range(2)
+                for g, n in enumerate(groups)
             ],
             axis=0,
         )
         acc = acc / total
         for c in range(LAT // 128):
-            latent_ref[c, pl.ds(i * pairs, pairs), :] = acc[:, c * 128:(c + 1) * 128]
-        stat_ref[pl.ds(i * pairs, pairs), :] = jnp.broadcast_to(
+            latent_ref[c, here, :] = acc[:, c * 128:(c + 1) * 128]
+        stat_ref[here, :] = jnp.broadcast_to(
             peak * SCALE + jnp.log(total), (pairs, 128)
         )
 
-    for i in range(TILES - 1):
-        tile(i)
-    pl.when(used == TILES)(lambda: tile(TILES - 1))
+    border = first // TILE * TILE
+    tile(CHIPS, SPARE, jnp.where(first - border <= SPARE, 0, 1))
+    for i in range(CHIPS // TILE):
+        tile(i * TILE, TILE, jnp.where(i * TILE + SPARE >= first, 1, 0))
     for h in range(0, HEADS, 2):
         rows = jnp.concatenate(
             [
@@ -345,7 +355,6 @@
     zero = jnp.zeros((), jnp.int32)
     place = [(chip * 2 + core) * 32, (chip * 2 + 1 - core) * 32, core, chip, lax.axis_index("y")]
     facts = jnp.concatenate([jnp.stack(place + [zero] * 3), prompt_ids, suffix_len])
-    facts, queries = lax.optimization_barrier((facts, queries))
     own = jnp.transpose(prompt_cache, (0, 2, 1))
     peer, suf_peer = swap(own), swap(suffix_cache)
     along_z = lax.all_to_all(pack(queries), "z", 0, 0, tiled=True)

time: 104 us -> 103 us (level)
  no operation moved by 1% of the time
where the time goes in v3:
time: 103 us
  blocking collectives  30.3 us (29%)
  waiting for transfers between devices  22.7 us (22%)
  starting transfers between devices  22 us (21%)
  Pallas kernels  20.3 us (20%)
  local copies, waits for them, and re-layouts  7.13 us (7%)
    pallas_call x6, Pallas kernels, call(): pl.pallas_call(kernel, out_shape=out, in_specs=specs, out_specs=out_specs...  20.3 us
    all_to_all x1, blocking collectives, per_device(): along_z = lax.all_to_all(pack(queries), 'z', 0, 0, tiled=True)  17.5 us
    all_to_all x1, blocking collectives, per_device(): return finish(lax.all_to_all(shares, ('c', 'x'), 0, 0, tiled=True)).T  12.8 us
    all_to_all x1, waiting for transfers between devices, per_device(): got = lax.all_to_all(parts, ('z', 'y'), 0, 0, tiled=True)  10.7 us
    all_to_all x1, waiting for transfers between devices, per_device(): values = lax.all_to_all(combine(facts, got), ('z', 'y'), 0, 0, tiled=True)  10.4 us
    all_to_all x1, starting transfers between devices, per_device(): got = lax.all_to_all(parts, ('z', 'y'), 0, 0, tiled=True)  7.27 us
    unnamed x10, local copies, waits for them, and re-layouts  6.38 us
    all_to_all x1, starting transfers between devices, per_device(): values = lax.all_to_all(combine(facts, got), ('z', 'y'), 0, 0, tiled=True)  5.15 us
  transfers between devices with their start and end apart: 8, of which 4 were waited for; matrix products, arithmetic and copies ran while one was open for 1% of the time, Pallas kernels for 4%

profile of v3, /device:TPU:1, one launch (start us, length us, event | category | flops | bytes accessed | tf_op | source)
XLA Modules:
  0.0 102.5 jit_solution(6546579258832218854)
XLA Ops:
  0.0 3.2 %collective-permute-start = (bf16[64,32,576]{2,1,0:T(8,128)(2,1)}, bf16[64,32,576]{2,1,0:T(8,128)(2,1)S(1)}, u32[]{:S(2)}, u32[]{:S(2)}) collective-permute-start(bf16[64,32,576]{2,1,0:T(8,128)(2,1)} %suf_own_ref.1), channel_id=1, source_target_pairs={{0,4},{4,0},{1,5},{5,1},{2,6},{6,2},{3,7},{7,3},{8,12},{12,8},{9,1... | collective-permute-start | bytes 7077896 | tf_op jit(solution)/shard_map/ppermute | solution.py:349
  3.2 0.0 collective-permute-start.4
  3.2 0.0 copy-start.4
  3.2 0.8 copy-done.4
  4.0 0.1 shard_map.73
  4.1 17.5 %all_to_all.20.q0_ref = bf16[8,144,128]{2,1,0:T(8,128)(2,1)S(1)} all-to-all(bf16[8,144,128]{2,1,0:T(8,128)(2,1)S(1)} %shard_map.73), channel_id=1, replica_groups=mesh['z'=8,'y'=4,'c'=2,'x'=4] {'z'}, dimensions={0} | all-to-all | bytes 589824 | tf_op jit(solution)/shard_map/all_to_all | solution.py:360
  21.6 0.0 collective-permute-done.suf_peer_ref
  21.6 1.3 %collective-permute-start.1 = (bf16[8,144,128]{2,1,0:T(8,128)(2,1)S(1)}, bf16[8,144,128]{2,1,0:T(8,128)(2,1)S(1)}, u32[]{:S(2)}, u32[]{:S(2)}) collective-permute-start(bf16[8,144,128]{2,1,0:T(8,128)(2,1)S(1)} %all_to_all.20.q0_ref), channel_id=1, source_target_pairs={{0,8},{8,16},{16,24},{24,0},{1,9},{9,17},{17,25},{25,1},{2,10},{10... | collective-permute-start | bytes 884744 | tf_op jit(solution)/shard_map/ppermute | solution.py:363
  22.9 2.6 %collective-permute-start.2 = (bf16[8,144,128]{2,1,0:T(8,128)(2,1)S(1)}, bf16[8,144,128]{2,1,0:T(8,128)(2,1)S(1)}, u32[]{:S(2)}, u32[]{:S(2)}) collective-permute-start(bf16[8,144,128]{2,1,0:T(8,128)(2,1)S(1)} %all_to_all.20.q0_ref), channel_id=1, source_target_pairs={{0,16},{8,24},{16,0},{24,8},{1,17},{9,25},{17,1},{25,9},{2,18},{10... | collective-permute-start | bytes 884744 | tf_op jit(solution)/shard_map/ppermute | solution.py:363
  25.5 1.1 %collective-permute-start.3 = (bf16[8,144,128]{2,1,0:T(8,128)(2,1)S(1)}, bf16[8,144,128]{2,1,0:T(8,128)(2,1)}, u32[]{:S(2)}, u32[]{:S(2)}) collective-permute-start(bf16[8,144,128]{2,1,0:T(8,128)(2,1)S(1)} %all_to_all.20.q0_ref), channel_id=1, source_target_pairs={{0,24},{8,0},{16,8},{24,16},{1,25},{9,1},{17,9},{25,17},{2,26},{10... | collective-permute-start | bytes 884744 | tf_op jit(solution)/shard_map/ppermute | solution.py:363
  26.6 0.8 concatenate.3.facts_ref
  27.4 0.0 copy-start
  27.4 2.2 %copy-done = bf16[32,512,128]{2,1,0:T(8,128)(2,1)S(1)} copy-done((bf16[32,512,128]{2,1,0:T(8,128)(2,1)S(1)}, bf16[32,512,128]{2,1,0:T(8,128)(2,1)}, u32[]{:S(2)}) %copy-start) | copy-done | bytes 4194328
  29.6 0.0 copy-start.1
  29.6 1.7 %copy-done.1 = bf16[64,32,576]{2,1,0:T(8,128)(2,1)S(1)} copy-done((bf16[64,32,576]{2,1,0:T(8,128)(2,1)S(1)}, bf16[64,32,576]{2,1,0:T(8,128)(2,1)}, u32[]{:S(2)}) %copy-start.1) | copy-done | bytes 2359320
  31.3 0.0 copy-start.2
  31.3 1.7 %copy-done.2 = bf16[2,1024,576]{1,2,0:T(8,128)(2,1)S(1)} copy-done((bf16[2,1024,576]{1,2,0:T(8,128)(2,1)S(1)}, bf16[2,1024,576]{1,2,0:T(8,128)(2,1)}, u32[]{:S(2)}) %copy-start.2) | copy-done | bytes 2359320
  33.0 2.2 %shard_map.74 = (s32[80]{0:T(128)S(1)}, bf16[9,256,576]{2,1,0:T(8,128)(2,1)S(1)}, bf16[2,576,1024]{2,1,0:T(8,128)(2,1)S(1)}, bf16[32,512,128]{2,1,0:T(8,128)(2,1)S(1)}) custom-call(s32[136]{0:T(256)S(1)} %concatenate.3.facts_ref, bf16[2,576,1024]{2,1,0:T(8,128)(2,1)S(1)} %bitcast.9, bf16[32,512,128]{2,1,0:T(8,128)(2,1)S(1)} %copy-done, ...), custom_call_target="tpu_custom_call" | custom-call | flops 268435456 | bytes 4194304 | tf_op jit(solution)/shard_map/pallas_call | solution.py:32
  35.2 0.0 collective-permute-done.4.peer_ref
  35.2 0.0 collective-permute-done.1.q1_ref
  35.2 1.5 %collective-permute-done.2.q2_ref = bf16[8,144,128]{2,1,0:T(8,128)(2,1)S(1)} collective-permute-done((bf16[8,144,128]{2,1,0:T(8,128)(2,1)S(1)}, bf16[8,144,128]{2,1,0:T(8,128)(2,1)S(1)}, u32[]{:S(2)}, u32[]{:S(2)}) %collective-permute-start.2) | collective-permute-done | bytes 294944 | tf_op jit(solution)/shard_map/ppermute | solution.py:363
  36.7 0.1 collective-permute-done.3.q3_ref
  36.8 0.0 copy-start.3
  36.8 14.2 %shard_map.75 = bf16[32,40,128]{2,1,0:T(8,128)(2,1)} custom-call(s32[136]{0:T(256)S(1)} %concatenate.3.facts_ref, s32[80]{0:T(128)S(1)} %get-tuple-element.14.table_ref, bf16[8,144,128]{2,1,0:T(8,128)(2,1)S(1)} %all_to_all.20.q0_ref, bf16[8,144,128]{2,1,0:T(8,128)(2,1)S(1)} %collective-permute-done.1.q1_ref, ...), custom_call_target="tpu_custom_call" | custom-call | flops 6127616000 | bytes 4194304 | tf_op jit(solution)/shard_map/pallas_call | solution.py:32
  51.0 7.3 %all-to-all-start.1 = ((bf16[32,40,128]{2,1,0:T(8,128)(2,1)}), bf16[32,40,128]{2,1,0:T(8,128)(2,1)S(1)}, u32[]{:S(2)}, u32[]{:S(2)}) async-start(bf16[32,40,128]{2,1,0:T(8,128)(2,1)} %shard_map.75), calls=%async_computation.1 | async-start | bytes 655360 | tf_op jit(solution)/shard_map/all_to_all | solution.py:369
  58.2 0.0 copy-done.3
  58.2 1.4 %collective-permute-start.5 = (bf16[112,4096]{1,0:T(8,128)(2,1)S(1)}, bf16[112,4096]{1,0:T(8,128)(2,1)S(1)}, u32[]{:S(2)}, u32[]{:S(2)}) collective-permute-start(bf16[112,4096]{1,0:T(8,128)(2,1)S(1)} %bitcast.10), channel_id=1, source_target_pairs={{0,4},{4,0},{1,5},{5,1},{2,6},{6,2},{3,7},{7,3},{8,12},{12,8},{9,1... | collective-permute-start | bytes 2752520 | tf_op jit(solution)/shard_map/ppermute | solution.py:349
  59.6 10.7 %all-to-all-done.1.got_ref = bf16[32,40,128]{2,1,0:T(8,128)(2,1)S(1)} async-done(((bf16[32,40,128]{2,1,0:T(8,128)(2,1)}), bf16[32,40,128]{2,1,0:T(8,128)(2,1)S(1)}, u32[]{:S(2)}, u32[]{:S(2)}) %all-to-all-start.1) | async-done | bytes 327712 | tf_op jit(solution)/shard_map/all_to_all | solution.py:369
  70.3 1.7 %shard_map.76 = bf16[32,32,128]{2,1,0:T(8,128)(2,1)} custom-call(s32[136]{0:T(256)S(1)} %concatenate.3.facts_ref, bf16[32,40,128]{2,1,0:T(8,128)(2,1)S(1)} %all-to-all-done.1.got_ref), custom_call_target="tpu_custom_call" | custom-call | flops 16777216 | bytes 4194304 | tf_op jit(solution)/shard_map/pallas_call | solution.py:32
  72.0 5.1 %all-to-all-start.2 = ((bf16[32,32,128]{2,1,0:T(8,128)(2,1)}), bf16[32,32,128]{2,1,0:T(8,128)(2,1)S(1)}, u32[]{:S(2)}, u32[]{:S(2)}) async-start(bf16[32,32,128]{2,1,0:T(8,128)(2,1)} %shard_map.76), calls=%async_computation.2 | async-start | bytes 524288 | tf_op jit(solution)/shard_map/all_to_all | solution.py:370
  77.2 0.0 collective-permute-done.5.peer_ref
  77.2 10.4 %all-to-all-done.2.values_ref = bf16[32,32,128]{2,1,0:T(8,128)(2,1)S(1)} async-done(((bf16[32,32,128]{2,1,0:T(8,128)(2,1)}), bf16[32,32,128]{2,1,0:T(8,128)(2,1)S(1)}, u32[]{:S(2)}, u32[]{:S(2)}) %all-to-all-start.2) | async-done | bytes 262176 | tf_op jit(solution)/shard_map/all_to_all | solution.py:370
  87.6 1.3 %shard_map.77 = f32[8,8,128]{2,1,0:T(8,128)S(1)} custom-call(s32[136]{0:T(256)S(1)} %concatenate.3.facts_ref, bf16[32,32,128]{2,1,0:T(8,128)(2,1)S(1)} %all-to-all-done.2.values_ref, bf16[112,4096]{1,0:T(8,128)(2,1)S(1)} %bitcast.11, bf16[112,4096]{1,0:T(8,128)(2,1)S(1)} %collective-permute-done.5.peer_ref), custom_call_target="tpu_custom_call" | custom-call | flops 134217728 | bytes 4194304 | tf_op jit(solution)/shard_map/pallas_call | solution.py:32
  88.9 12.8 %all_to_all.21.got_ref = f32[8,8,128]{2,1,0:T(8,128)S(1)} all-to-all(f32[8,8,128]{2,1,0:T(8,128)S(1)} %shard_map.77), channel_id=1, replica_groups=mesh['z'=8,'y'=4,'c'=2,'x'=4] {'c','x'}, dimensions={0} | all-to-all | bytes 65536 | tf_op jit(solution)/shard_map/all_to_all | solution.py:372
  101.7 0.9 shard_map.78
  (1 shorter events, 0.0 us)
Async XLA Ops:
  0.0 21.6 %collective-permute-start = (bf16[64,32,576]{2,1,0:T(8,128)(2,1)}, bf16[64,32,576]{2,1,0:T(8,128)(2,1)S(1)}, u32[]{:S(2)}, u32[]{:S(2)}) collective-permute-start(bf16[64,32,576]{2,1,0:T(8,128)(2,1)} %suf_own_ref.1), channel_id=1, source_target_pairs={{0,4},{4,0},{1,5},{5,1},{2,6},{6,2},{3,7},{7,3},{8,12},{12,8},{9,1... | collective-permute-start | bytes 7077896 | tf_op jit(solution)/shard_map/ppermute | solution.py:349
  3.2 31.9 %collective-permute-start.4 = (bf16[2,576,1024]{2,1,0:T(8,128)(2,1)}, bf16[2,576,1024]{2,1,0:T(8,128)(2,1)}, u32[]{:S(2)}, u32[]{:S(2)}) collective-permute-start(bf16[2,576,1024]{2,1,0:T(8,128)(2,1)} %bitcast.8), channel_id=1, source_target_pairs={{0,4},{4,0},{1,5},{5,1},{2,6},{6,2},{3,7},{7,3},{8,12},{12,8},{9,1... | collective-permute-start | bytes 7077896 | tf_op jit(solution)/shard_map/ppermute | solution.py:349
  3.2 0.8 copy-start.4
  21.6 13.6 %collective-permute-start.1 = (bf16[8,144,128]{2,1,0:T(8,128)(2,1)S(1)}, bf16[8,144,128]{2,1,0:T(8,128)(2,1)S(1)}, u32[]{:S(2)}, u32[]{:S(2)}) collective-permute-start(bf16[8,144,128]{2,1,0:T(8,128)(2,1)S(1)} %all_to_all.20.q0_ref), channel_id=1, source_target_pairs={{0,8},{8,16},{16,24},{24,0},{1,9},{9,17},{17,25},{25,1},{2,10},{10... | collective-permute-start | bytes 884744 | tf_op jit(solution)/shard_map/ppermute | solution.py:363
  22.9 13.7 %collective-permute-start.2 = (bf16[8,144,128]{2,1,0:T(8,128)(2,1)S(1)}, bf16[8,144,128]{2,1,0:T(8,128)(2,1)S(1)}, u32[]{:S(2)}, u32[]{:S(2)}) collective-permute-start(bf16[8,144,128]{2,1,0:T(8,128)(2,1)S(1)} %all_to_all.20.q0_ref), channel_id=1, source_target_pairs={{0,16},{8,24},{16,0},{24,8},{1,17},{9,25},{17,1},{25,9},{2,18},{10... | collective-permute-start | bytes 884744 | tf_op jit(solution)/shard_map/ppermute | solution.py:363
  25.5 11.3 %collective-permute-start.3 = (bf16[8,144,128]{2,1,0:T(8,128)(2,1)S(1)}, bf16[8,144,128]{2,1,0:T(8,128)(2,1)}, u32[]{:S(2)}, u32[]{:S(2)}) collective-permute-start(bf16[8,144,128]{2,1,0:T(8,128)(2,1)S(1)} %all_to_all.20.q0_ref), channel_id=1, source_target_pairs={{0,24},{8,0},{16,8},{24,16},{1,25},{9,1},{17,9},{25,17},{2,26},{10... | collective-permute-start | bytes 884744 | tf_op jit(solution)/shard_map/ppermute | solution.py:363
  27.4 2.2 %copy-start = (bf16[32,512,128]{2,1,0:T(8,128)(2,1)S(1)}, bf16[32,512,128]{2,1,0:T(8,128)(2,1)}, u32[]{:S(2)}) copy-start(bf16[32,512,128]{2,1,0:T(8,128)(2,1)} %uv_in.1) | copy-start | bytes 12582916
  29.6 1.7 %copy-start.1 = (bf16[64,32,576]{2,1,0:T(8,128)(2,1)S(1)}, bf16[64,32,576]{2,1,0:T(8,128)(2,1)}, u32[]{:S(2)}) copy-start(bf16[64,32,576]{2,1,0:T(8,128)(2,1)} %suf_own_ref.1) | copy-start | bytes 7077892
  31.3 1.7 %copy-start.2 = (bf16[2,1024,576]{1,2,0:T(8,128)(2,1)S(1)}, bf16[2,1024,576]{1,2,0:T(8,128)(2,1)}, u32[]{:S(2)}) copy-start(bf16[2,1024,576]{1,2,0:T(8,128)(2,1)} %param.8) | copy-start | bytes 7077892
  36.8 21.4 %copy-start.3 = (bf16[4096,112]{0,1:T(8,128)(2,1)S(1)}, bf16[4096,112]{0,1:T(8,128)(2,1)}, u32[]{:S(2)}) copy-start(bf16[4096,112]{0,1:T(8,128)(2,1)} %param.13) | copy-start | bytes 2752516
  51.0 19.4 %all-to-all-start.1 = ((bf16[32,40,128]{2,1,0:T(8,128)(2,1)}), bf16[32,40,128]{2,1,0:T(8,128)(2,1)S(1)}, u32[]{:S(2)}, u32[]{:S(2)}) async-start(bf16[32,40,128]{2,1,0:T(8,128)(2,1)} %shard_map.75), calls=%async_computation.1 | async-start | bytes 655360 | tf_op jit(solution)/shard_map/all_to_all | solution.py:369
  58.2 19.0 %collective-permute-start.5 = (bf16[112,4096]{1,0:T(8,128)(2,1)S(1)}, bf16[112,4096]{1,0:T(8,128)(2,1)S(1)}, u32[]{:S(2)}, u32[]{:S(2)}) collective-permute-start(bf16[112,4096]{1,0:T(8,128)(2,1)S(1)} %bitcast.10), channel_id=1, source_target_pairs={{0,4},{4,0},{1,5},{5,1},{2,6},{6,2},{3,7},{7,3},{8,12},{12,8},{9,1... | collective-permute-start | bytes 2752520 | tf_op jit(solution)/shard_map/ppermute | solution.py:349
  72.0 15.6 %all-to-all-start.2 = ((bf16[32,32,128]{2,1,0:T(8,128)(2,1)}), bf16[32,32,128]{2,1,0:T(8,128)(2,1)S(1)}, u32[]{:S(2)}, u32[]{:S(2)}) async-start(bf16[32,32,128]{2,1,0:T(8,128)(2,1)} %shard_map.76), calls=%async_computation.2 | async-start | bytes 524288 | tf_op jit(solution)/shard_map/all_to_all | solution.py:370

commit v4 on v3

--- a/solution.py
+++ b/solution.py
@@ -71,14 +71,11 @@
 
 
 def prepare_kernel(
-    facts_ref, own_in, uv_in, suf_own_ref, suf_peer_ref, table_ref, keys_ref, own_ref, uv_ref, sem
+    facts_ref, own_in, peer_in, uv_in, suf_own_ref, suf_peer_ref, table_ref, keys_ref, peer_ref, sem
 ):
-    copies = [
-        pltpu.make_async_copy(own_in, own_ref, sem.at[0]),
-        pltpu.make_async_copy(uv_in, uv_ref, sem.at[1]),
-    ]
-    for copy in copies:
-        copy.start()
+    del own_in, uv_in
+    copy = pltpu.make_async_copy(peer_in, peer_ref, sem)
+    copy.start()
     core = facts_ref[2]
     first = jnp.int32(0)
     for t in range(CHIPS):
@@ -107,26 +104,24 @@
         t = table_ref[CHIPS + s]
         keys_ref[s // 4, pl.ds(s % 4 * KEYS, 32), :] = suf_own_ref[2 * t + core]
         keys_ref[s // 4, pl.ds(s % 4 * KEYS + 32, 32), :] = suf_peer_ref[2 * t + core]
-    for copy in copies:
-        copy.wait()
-
-
-def prepare(facts, own, uv, suf_own, suf_peer):
+    copy.wait()
+
+
+def prepare(facts, own, peer, uv, suf_own, suf_peer):
     away = pl.BlockSpec(memory_space=pl.ANY)
     return call(
         prepare_kernel,
         (
             jax.ShapeDtypeStruct((CHIPS + SLOTS + 8,), jnp.int32),
             jax.ShapeDtypeStruct((USED // 4, 4 * KEYS, LAT + ROPE), jnp.bfloat16),
-            jax.ShapeDtypeStruct(own.shape, own.dtype),
-            jax.ShapeDtypeStruct(uv.shape, uv.dtype),
+            jax.ShapeDtypeStruct(peer.shape, peer.dtype),
         ),
-        [SMEM, away, away, BLOCK, BLOCK],
-        (SMEM, BLOCK, BLOCK, BLOCK),
-        [pltpu.SemaphoreType.DMA((2,))],
+        [SMEM, away, away, away, BLOCK, BLOCK],
+        (SMEM, BLOCK, BLOCK),
+        [pltpu.SemaphoreType.DMA],
         20,
         2**28,
-        facts, own, uv, suf_own, suf_peer,
+        facts, own, peer, uv, suf_own, suf_peer,
     )
 
 
@@ -252,7 +247,7 @@
             pltpu.VMEM((pairs, VH), jnp.float32),
             pltpu.VMEM((pairs, 128), jnp.float32),
         ],
-        30,
+        22,
         2 * pairs * 2200 * 1088,
         facts, table, *qs, own, peer, keys, uv,
     )
@@ -362,10 +357,10 @@
     qs = [along_z] + [
         lax.ppermute(along_z, "y", [(i, (i + j) % NY) for i in range(NY)]) for j in range(1, NY)
     ]
-    table, keys, own, uv = prepare(facts, own, w_uv, suffix_cache, suf_peer)
-    parts = attend(facts, table, qs, own, peer, keys, uv)
-    parts, w_t = lax.optimization_barrier((parts, w_out.T))
-    w_peer = swap(w_t)
+    table, keys, peer = prepare(facts, own, peer, w_uv, suffix_cache, suf_peer)
+    qs, keys, w_t = lax.optimization_barrier((qs, keys, w_out.T))
+    parts = attend(facts, table, qs, own, peer, keys, w_uv)
+    parts, w_peer = lax.optimization_barrier((parts, swap(w_t)))
     got = lax.all_to_all(parts, ("z", "y"), 0, 0, tiled=True)
     values = lax.all_to_all(combine(facts, got), ("z", "y"), 0, 0, tiled=True)
     shares = project(facts, values, w_t, w_peer)

time: 103 us -> 101 us (0.981)
  blocking collectives: 30.3 us -> 62.9 us
  waiting for transfers between devices: 22.7 us -> 0.74 us
  starting transfers between devices: 22 us -> 11.3 us
  Pallas kernels: 20.3 us -> 19 us
    all_to_all x0 -> x2, blocking collectives: none -> 32.8 us  [the longest x1 18.2 us: per_device(): got = lax.all_to_all(parts, ('z', 'y'), 0, 0, tiled=True)]
    all_to_all x2 -> x0, waiting for transfers between devices: 21.1 us -> none  [the longest x1 10.7 us: per_device(): got = lax.all_to_all(parts, ('z', 'y'), 0, 0, tiled=True)]
    all_to_all x2 -> x0, starting transfers between devices: 12.4 us -> none  [the longest x1 7.27 us: per_device(): got = lax.all_to_all(parts, ('z', 'y'), 0, 0, tiled=True)]
    ppermute x3, starting transfers between devices: 4.62 us -> 6.27 us  [swap(): return lax.ppermute(x, 'c', [(0, 1), (1, 0)])]
    pallas_call x6, Pallas kernels: 20.3 us -> 19 us  [call(): pl.pallas_call(kernel, out_shape=out, in_specs=specs, out_specs=out_specs...]
    unnamed x10 -> x14, local copies, waits for them, and re-layouts: 6.38 us -> 6.38 us
  transfers between devices with their start and end apart: 8 -> 6, of which waited for: 4 -> 2; matrix products, arithmetic and copies ran while one was open for 1% -> 1% of each run, Pallas kernels for 4% -> 16%
where the time goes in v4:
time: 101 us
  blocking collectives  62.9 us (62%)
  Pallas kernels  19 us (19%)
  starting transfers between devices  11.3 us (11%)
  local copies, waits for them, and re-layouts  7.13 us (7%)
    pallas_call x6, Pallas kernels, call(): pl.pallas_call(kernel, out_shape=out, in_specs=specs, out_specs=out_specs...  19 us
    all_to_all x1, blocking collectives, per_device(): got = lax.all_to_all(parts, ('z', 'y'), 0, 0, tiled=True)  18.2 us
    all_to_all x1, blocking collectives, per_device(): along_z = lax.all_to_all(pack(queries), 'z', 0, 0, tiled=True)  17.5 us
    all_to_all x1, blocking collectives, per_device(): values = lax.all_to_all(combine(facts, got), ('z', 'y'), 0, 0, tiled=True)  14.5 us
    all_to_all x1, blocking collectives, per_device(): return finish(lax.all_to_all(shares, ('c', 'x'), 0, 0, tiled=True)).T  12.6 us
    unnamed x14, local copies, waits for them, and re-layouts  6.38 us
    ppermute x3, starting transfers between devices, swap(): return lax.ppermute(x, 'c', [(0, 1), (1, 0)])  6.27 us
    ppermute x3, starting transfers between devices, per_device(): lax.ppermute(along_z, 'y', [(i, (i + j) % NY) for i in range(NY)])  4.99 us
  transfers between devices with their start and end apart: 6, of which 2 were waited for; matrix products, arithmetic and copies ran while one was open for 1% of the time, Pallas kernels for 16%

profile of v4, /device:TPU:1, one launch (start us, length us, event | category | flops | bytes accessed | tf_op | source)
XLA Modules:
  0.0 101.1 jit_solution(6169204958574458486)
XLA Ops:
  0.0 3.2 %collective-permute-start.1 = (bf16[64,32,576]{2,1,0:T(8,128)(2,1)}, bf16[64,32,576]{2,1,0:T(8,128)(2,1)S(1)}, u32[]{:S(2)}, u32[]{:S(2)}) collective-permute-start(bf16[64,32,576]{2,1,0:T(8,128)(2,1)} %suf_own_ref.1), channel_id=1, source_target_pairs={{0,4},{4,0},{1,5},{5,1},{2,6},{6,2},{3,7},{7,3},{8,12},{12,8},{9,1... | collective-permute-start | bytes 7077896 | tf_op jit(solution)/shard_map/ppermute | solution.py:344
  3.2 0.0 collective-permute-start
  3.2 0.0 copy-start.6
  3.2 0.8 copy-done.6
  4.0 0.1 shard_map.73
  4.1 17.5 %all_to_all.20.q0_ref = bf16[8,144,128]{2,1,0:T(8,128)(2,1)S(1)} all-to-all(bf16[8,144,128]{2,1,0:T(8,128)(2,1)S(1)} %shard_map.73), channel_id=1, replica_groups=mesh['z'=8,'y'=4,'c'=2,'x'=4] {'z'}, dimensions={0} | all-to-all | bytes 589824 | tf_op jit(solution)/shard_map/all_to_all | solution.py:355
  21.6 0.0 collective-permute-done.1.suf_peer_ref
  21.6 1.3 %collective-permute-start.2 = (bf16[8,144,128]{2,1,0:T(8,128)(2,1)S(1)}, bf16[8,144,128]{2,1,0:T(8,128)(2,1)S(1)}, u32[]{:S(2)}, u32[]{:S(2)}) collective-permute-start(bf16[8,144,128]{2,1,0:T(8,128)(2,1)S(1)} %all_to_all.20.q0_ref), channel_id=1, source_target_pairs={{0,8},{8,16},{16,24},{24,0},{1,9},{9,17},{17,25},{25,1},{2,10},{10... | collective-permute-start | bytes 884744 | tf_op jit(solution)/shard_map/ppermute | solution.py:358
  22.9 2.6 %collective-permute-start.3 = (bf16[8,144,128]{2,1,0:T(8,128)(2,1)S(1)}, bf16[8,144,128]{2,1,0:T(8,128)(2,1)S(1)}, u32[]{:S(2)}, u32[]{:S(2)}) collective-permute-start(bf16[8,144,128]{2,1,0:T(8,128)(2,1)S(1)} %all_to_all.20.q0_ref), channel_id=1, source_target_pairs={{0,16},{8,24},{16,0},{24,8},{1,17},{9,25},{17,1},{25,9},{2,18},{10... | collective-permute-start | bytes 884744 | tf_op jit(solution)/shard_map/ppermute | solution.py:358
  25.5 1.1 %collective-permute-start.4 = (bf16[8,144,128]{2,1,0:T(8,128)(2,1)S(1)}, bf16[8,144,128]{2,1,0:T(8,128)(2,1)}, u32[]{:S(2)}, u32[]{:S(2)}) collective-permute-start(bf16[8,144,128]{2,1,0:T(8,128)(2,1)S(1)} %all_to_all.20.q0_ref), channel_id=1, source_target_pairs={{0,24},{8,0},{16,8},{24,16},{1,25},{9,1},{17,9},{25,17},{2,26},{10... | collective-permute-start | bytes 884744 | tf_op jit(solution)/shard_map/ppermute | solution.py:358
  26.6 0.8 concatenate.3.facts_ref
  27.4 0.0 collective-permute-done.peer_in
  27.4 0.0 copy-start
  27.4 2.2 %copy-done = bf16[32,512,128]{2,1,0:T(8,128)(2,1)S(1)} copy-done((bf16[32,512,128]{2,1,0:T(8,128)(2,1)S(1)}, bf16[32,512,128]{2,1,0:T(8,128)(2,1)}, u32[]{:S(2)}) %copy-start) | copy-done | bytes 4194328
  29.6 0.0 copy-start.2
  29.6 1.7 %copy-done.2 = bf16[64,32,576]{2,1,0:T(8,128)(2,1)S(1)} copy-done((bf16[64,32,576]{2,1,0:T(8,128)(2,1)S(1)}, bf16[64,32,576]{2,1,0:T(8,128)(2,1)}, u32[]{:S(2)}) %copy-start.2) | copy-done | bytes 2359320
  31.3 0.0 copy-start.3
  31.3 1.7 %copy-done.3 = bf16[2,1024,576]{1,2,0:T(8,128)(2,1)S(1)} copy-done((bf16[2,1024,576]{1,2,0:T(8,128)(2,1)S(1)}, bf16[2,1024,576]{1,2,0:T(8,128)(2,1)}, u32[]{:S(2)}) %copy-start.3) | copy-done | bytes 2359320
  33.0 0.0 copy-start.5
  33.0 0.0 copy-start.1
  33.0 0.0 copy-start.4
  33.0 3.1 %shard_map.74 = (s32[80]{0:T(128)S(1)}, bf16[9,256,576]{2,1,0:T(8,128)(2,1)S(1)}, bf16[2,576,1024]{2,1,0:T(8,128)(2,1)S(1)}) custom-call(s32[136]{0:T(256)S(1)} %concatenate.3.facts_ref, bf16[2,576,1024]{2,1,0:T(8,128)(2,1)S(1)} %bitcast.9, bf16[2,576,1024]{2,1,0:T(8,128)(2,1)} %collective-permute-done.peer_in, bf16[32,512,128]{2,1,0:T(8,128)(2,1)S(1)} %copy-done, ...), custom_call_target="tpu_custom_call" | custom-call | flops 268435456 | bytes 4194304 | tf_op jit(solution)/shard_map/pallas_call | solution.py:32
  36.1 0.0 collective-permute-done.2.q1_ref
  36.1 0.6 collective-permute-done.3.q2_ref
  36.7 0.1 collective-permute-done.4.q3_ref
  36.8 0.0 copy-done.5
  36.8 3.0 %collective-permute-start.5 = (bf16[112,4096]{1,0:T(8,128)(2,1)S(1)}, bf16[112,4096]{1,0:T(8,128)(2,1)S(1)}, u32[]{:S(2)}, u32[]{:S(2)}) collective-permute-start(bf16[112,4096]{1,0:T(8,128)(2,1)S(1)} %bitcast.11), channel_id=1, source_target_pairs={{0,4},{4,0},{1,5},{5,1},{2,6},{6,2},{3,7},{7,3},{8,12},{12,8},{9,1... | collective-permute-start | bytes 2752520 | tf_op jit(solution)/shard_map/ppermute | solution.py:344
  39.8 0.0 copy-done.1
  39.8 0.0 copy-done.4
  39.8 12.6 %shard_map.75 = bf16[32,40,128]{2,1,0:T(8,128)(2,1)S(1)} custom-call(s32[136]{0:T(256)S(1)} %concatenate.3.facts_ref, s32[80]{0:T(128)S(1)} %get-tuple-element.19.table_ref, bf16[8,144,128]{2,1,0:T(8,128)(2,1)S(1)} %all_to_all.20.q0_ref, bf16[8,144,128]{2,1,0:T(8,128)(2,1)S(1)} %collective-permute-done.2.q1_ref, ...), custom_call_target="tpu_custom_call" | custom-call | flops 6127616000 | bytes 4194304 | tf_op jit(solution)/shard_map/pallas_call | solution.py:32
  52.5 0.0 collective-permute-done.5.peer_ref
  52.5 18.2 %all_to_all.21.got_ref = bf16[32,40,128]{2,1,0:T(8,128)(2,1)S(1)} all-to-all(bf16[32,40,128]{2,1,0:T(8,128)(2,1)S(1)} %shard_map.75), channel_id=1, replica_groups=mesh['z'=8,'y'=4,'c'=2,'x'=4] {'z','y'}, dimensions={0} | all-to-all | bytes 655360 | tf_op jit(solution)/shard_map/all_to_all | solution.py:364
  70.7 1.0 %shard_map.76 = bf16[32,32,128]{2,1,0:T(8,128)(2,1)S(1)} custom-call(s32[136]{0:T(256)S(1)} %concatenate.3.facts_ref, bf16[32,40,128]{2,1,0:T(8,128)(2,1)S(1)} %all_to_all.21.got_ref), custom_call_target="tpu_custom_call" | custom-call | flops 16777216 | bytes 4194304 | tf_op jit(solution)/shard_map/pallas_call | solution.py:32
  71.7 14.5 %all_to_all.22.values_ref = bf16[32,32,128]{2,1,0:T(8,128)(2,1)S(1)} all-to-all(bf16[32,32,128]{2,1,0:T(8,128)(2,1)S(1)} %shard_map.76), channel_id=1, replica_groups=mesh['z'=8,'y'=4,'c'=2,'x'=4] {'z','y'}, dimensions={0} | all-to-all | bytes 524288 | tf_op jit(solution)/shard_map/all_to_all | solution.py:365
  86.3 1.3 %shard_map.77 = f32[8,8,128]{2,1,0:T(8,128)S(1)} custom-call(s32[136]{0:T(256)S(1)} %concatenate.3.facts_ref, bf16[32,32,128]{2,1,0:T(8,128)(2,1)S(1)} %all_to_all.22.values_ref, bf16[112,4096]{1,0:T(8,128)(2,1)S(1)} %bitcast.12, bf16[112,4096]{1,0:T(8,128)(2,1)S(1)} %collective-permute-done.5.peer_ref), custom_call_target="tpu_custom_call" | custom-call | flops 134217728 | bytes 4194304 | tf_op jit(solution)/shard_map/pallas_call | solution.py:32
  87.6 12.6 %all_to_all.23.got_ref = f32[8,8,128]{2,1,0:T(8,128)S(1)} all-to-all(f32[8,8,128]{2,1,0:T(8,128)S(1)} %shard_map.77), channel_id=1, replica_groups=mesh['z'=8,'y'=4,'c'=2,'x'=4] {'c','x'}, dimensions={0} | all-to-all | bytes 65536 | tf_op jit(solution)/shard_map/all_to_all | solution.py:367
  100.2 0.9 shard_map.78
  (1 shorter events, 0.0 us)
Async XLA Ops:
  0.0 21.6 %collective-permute-start.1 = (bf16[64,32,576]{2,1,0:T(8,128)(2,1)}, bf16[64,32,576]{2,1,0:T(8,128)(2,1)S(1)}, u32[]{:S(2)}, u32[]{:S(2)}) collective-permute-start(bf16[64,32,576]{2,1,0:T(8,128)(2,1)} %suf_own_ref.1), channel_id=1, source_target_pairs={{0,4},{4,0},{1,5},{5,1},{2,6},{6,2},{3,7},{7,3},{8,12},{12,8},{9,1... | collective-permute-start | bytes 7077896 | tf_op jit(solution)/shard_map/ppermute | solution.py:344
  3.2 24.1 %collective-permute-start = (bf16[2,576,1024]{2,1,0:T(8,128)(2,1)}, bf16[2,576,1024]{2,1,0:T(8,128)(2,1)}, u32[]{:S(2)}, u32[]{:S(2)}) collective-permute-start(bf16[2,576,1024]{2,1,0:T(8,128)(2,1)} %bitcast.8), channel_id=1, source_target_pairs={{0,4},{4,0},{1,5},{5,1},{2,6},{6,2},{3,7},{7,3},{8,12},{12,8},{9,1... | collective-permute-start | bytes 7077896 | tf_op jit(solution)/shard_map/ppermute | solution.py:344
  3.2 0.8 copy-start.6
  21.6 14.4 %collective-permute-start.2 = (bf16[8,144,128]{2,1,0:T(8,128)(2,1)S(1)}, bf16[8,144,128]{2,1,0:T(8,128)(2,1)S(1)}, u32[]{:S(2)}, u32[]{:S(2)}) collective-permute-start(bf16[8,144,128]{2,1,0:T(8,128)(2,1)S(1)} %all_to_all.20.q0_ref), channel_id=1, source_target_pairs={{0,8},{8,16},{16,24},{24,0},{1,9},{9,17},{17,25},{25,1},{2,10},{10... | collective-permute-start | bytes 884744 | tf_op jit(solution)/shard_map/ppermute | solution.py:358
  22.9 13.7 %collective-permute-start.3 = (bf16[8,144,128]{2,1,0:T(8,128)(2,1)S(1)}, bf16[8,144,128]{2,1,0:T(8,128)(2,1)S(1)}, u32[]{:S(2)}, u32[]{:S(2)}) collective-permute-start(bf16[8,144,128]{2,1,0:T(8,128)(2,1)S(1)} %all_to_all.20.q0_ref), channel_id=1, source_target_pairs={{0,16},{8,24},{16,0},{24,8},{1,17},{9,25},{17,1},{25,9},{2,18},{10... | collective-permute-start | bytes 884744 | tf_op jit(solution)/shard_map/ppermute | solution.py:358
  25.5 11.3 %collective-permute-start.4 = (bf16[8,144,128]{2,1,0:T(8,128)(2,1)S(1)}, bf16[8,144,128]{2,1,0:T(8,128)(2,1)}, u32[]{:S(2)}, u32[]{:S(2)}) collective-permute-start(bf16[8,144,128]{2,1,0:T(8,128)(2,1)S(1)} %all_to_all.20.q0_ref), channel_id=1, source_target_pairs={{0,24},{8,0},{16,8},{24,16},{1,25},{9,1},{17,9},{25,17},{2,26},{10... | collective-permute-start | bytes 884744 | tf_op jit(solution)/shard_map/ppermute | solution.py:358
  27.4 2.2 %copy-start = (bf16[32,512,128]{2,1,0:T(8,128)(2,1)S(1)}, bf16[32,512,128]{2,1,0:T(8,128)(2,1)}, u32[]{:S(2)}) copy-start(bf16[32,512,128]{2,1,0:T(8,128)(2,1)} %uv_ref.1) | copy-start | bytes 12582916
  29.6 1.7 %copy-start.2 = (bf16[64,32,576]{2,1,0:T(8,128)(2,1)S(1)}, bf16[64,32,576]{2,1,0:T(8,128)(2,1)}, u32[]{:S(2)}) copy-start(bf16[64,32,576]{2,1,0:T(8,128)(2,1)} %suf_own_ref.1) | copy-start | bytes 7077892
  31.3 1.7 %copy-start.3 = (bf16[2,1024,576]{1,2,0:T(8,128)(2,1)S(1)}, bf16[2,1024,576]{1,2,0:T(8,128)(2,1)}, u32[]{:S(2)}) copy-start(bf16[2,1024,576]{1,2,0:T(8,128)(2,1)} %param.8) | copy-start | bytes 7077892
  33.0 3.8 %copy-start.5 = (bf16[4096,112]{0,1:T(8,128)(2,1)S(1)}, bf16[4096,112]{0,1:T(8,128)(2,1)}, u32[]{:S(2)}) copy-start(bf16[4096,112]{0,1:T(8,128)(2,1)} %param.13) | copy-start | bytes 2752516
  33.0 6.9 %copy-start.1 = (bf16[32,512,128]{2,1,0:T(8,128)(2,1)S(1)}, bf16[32,512,128]{2,1,0:T(8,128)(2,1)}, u32[]{:S(2)}) copy-start(bf16[32,512,128]{2,1,0:T(8,128)(2,1)} %uv_ref.1) | copy-start | bytes 12582916
  33.0 6.9 %copy-start.4 = (bf16[2,1024,576]{1,2,0:T(8,128)(2,1)S(1)}, bf16[2,1024,576]{1,2,0:T(8,128)(2,1)}, u32[]{:S(2)}) copy-start(bf16[2,1024,576]{1,2,0:T(8,128)(2,1)} %param.8) | copy-start | bytes 7077892
  36.8 15.7 %collective-permute-start.5 = (bf16[112,4096]{1,0:T(8,128)(2,1)S(1)}, bf16[112,4096]{1,0:T(8,128)(2,1)S(1)}, u32[]{:S(2)}, u32[]{:S(2)}) collective-permute-start(bf16[112,4096]{1,0:T(8,128)(2,1)S(1)} %bitcast.11), channel_id=1, source_target_pairs={{0,4},{4,0},{1,5},{5,1},{2,6},{6,2},{3,7},{7,3},{8,12},{12,8},{9,1... | collective-permute-start | bytes 2752520 | tf_op jit(solution)/shard_map/ppermute | solution.py:344

commit v5 on v4

--- a/solution.py
+++ b/solution.py
@@ -358,11 +358,12 @@
         lax.ppermute(along_z, "y", [(i, (i + j) % NY) for i in range(NY)]) for j in range(1, NY)
     ]
     table, keys, peer = prepare(facts, own, peer, w_uv, suffix_cache, suf_peer)
-    qs, keys, w_t = lax.optimization_barrier((qs, keys, w_out.T))
+    qs, keys = lax.optimization_barrier((qs, keys))
     parts = attend(facts, table, qs, own, peer, keys, w_uv)
-    parts, w_peer = lax.optimization_barrier((parts, swap(w_t)))
     got = lax.all_to_all(parts, ("z", "y"), 0, 0, tiled=True)
-    values = lax.all_to_all(combine(facts, got), ("z", "y"), 0, 0, tiled=True)
+    mine, w_t = lax.optimization_barrier((combine(facts, got), w_out.T))
+    w_peer = swap(w_t)
+    values = lax.all_to_all(mine, ("z", "y"), 0, 0, tiled=True)
     shares = project(facts, values, w_t, w_peer)
     return finish(lax.all_to_all(shares, ("c", "x"), 0, 0, tiled=True)).T
 

time: 101 us -> 102 us (level)
    all_to_all x1, blocking collectives: 12.6 us -> 11 us  [per_device(): return finish(lax.all_to_all(shares, ('c', 'x'), 0, 0, tiled=True)).T]
    all_to_all x1, blocking collectives: 14.5 us -> 15.7 us  [per_device(): values = lax.all_to_all(mine, ('z', 'y'), 0, 0, tiled=True)]
  transfers between devices with their start and end apart: 6 -> 6, of which waited for: 2 -> 2; matrix products, arithmetic and copies ran while one was open for 1% -> 1% of each run, Pallas kernels for 16% -> 3%
where the time goes in v5:
time: 102 us
  blocking collectives  63.5 us (62%)
  Pallas kernels  19.1 us (19%)
  starting transfers between devices  11.1 us (11%)
  local copies, waits for them, and re-layouts  7.13 us (7%)
    all_to_all x1, blocking collectives, per_device(): got = lax.all_to_all(parts, ('z', 'y'), 0, 0, tiled=True)  19.2 us
    pallas_call x6, Pallas kernels, call(): pl.pallas_call(kernel, out_shape=out, in_specs=specs, out_specs=out_specs...  19.1 us
    all_to_all x1, blocking collectives, per_device(): along_z = lax.all_to_all(pack(queries), 'z', 0, 0, tiled=True)  17.5 us
    all_to_all x1, blocking collectives, per_device(): values = lax.all_to_all(mine, ('z', 'y'), 0, 0, tiled=True)  15.7 us
    all_to_all x1, blocking collectives, per_device(): return finish(lax.all_to_all(shares, ('c', 'x'), 0, 0, tiled=True)).T  11 us
    unnamed x14, local copies, waits for them, and re-layouts  6.38 us
    ppermute x3, starting transfers between devices, swap(): return lax.ppermute(x, 'c', [(0, 1), (1, 0)])  6.13 us
    ppermute x3, starting transfers between devices, per_device(): lax.ppermute(along_z, 'y', [(i, (i + j) % NY) for i in range(NY)])  4.99 us
  transfers between devices with their start and end apart: 6, of which 2 were waited for; matrix products, arithmetic and copies ran while one was open for 1% of the time, Pallas kernels for 3%

profile of v5, /device:TPU:1, one launch (start us, length us, event | category | flops | bytes accessed | tf_op | source)
XLA Modules:
  0.0 101.6 jit_solution(708412875406188385)
XLA Ops:
  0.0 3.2 %collective-permute-start.1 = (bf16[64,32,576]{2,1,0:T(8,128)(2,1)}, bf16[64,32,576]{2,1,0:T(8,128)(2,1)S(1)}, u32[]{:S(2)}, u32[]{:S(2)}) collective-permute-start(bf16[64,32,576]{2,1,0:T(8,128)(2,1)} %suf_own_ref.1), channel_id=1, source_target_pairs={{0,4},{4,0},{1,5},{5,1},{2,6},{6,2},{3,7},{7,3},{8,12},{12,8},{9,1... | collective-permute-start | bytes 7077896 | tf_op jit(solution)/shard_map/ppermute | solution.py:344
  3.2 0.0 collective-permute-start
  3.2 0.0 copy-start.6
  3.2 0.8 copy-done.6
  4.0 0.1 shard_map.73
  4.1 17.5 %all_to_all.20.q0_ref = bf16[8,144,128]{2,1,0:T(8,128)(2,1)S(1)} all-to-all(bf16[8,144,128]{2,1,0:T(8,128)(2,1)S(1)} %shard_map.73), channel_id=1, replica_groups=mesh['z'=8,'y'=4,'c'=2,'x'=4] {'z'}, dimensions={0} | all-to-all | bytes 589824 | tf_op jit(solution)/shard_map/all_to_all | solution.py:355
  21.6 0.0 collective-permute-done.1.suf_peer_ref
  21.6 1.3 %collective-permute-start.2 = (bf16[8,144,128]{2,1,0:T(8,128)(2,1)S(1)}, bf16[8,144,128]{2,1,0:T(8,128)(2,1)S(1)}, u32[]{:S(2)}, u32[]{:S(2)}) collective-permute-start(bf16[8,144,128]{2,1,0:T(8,128)(2,1)S(1)} %all_to_all.20.q0_ref), channel_id=1, source_target_pairs={{0,8},{8,16},{16,24},{24,0},{1,9},{9,17},{17,25},{25,1},{2,10},{10... | collective-permute-start | bytes 884744 | tf_op jit(solution)/shard_map/ppermute | solution.py:358
  22.9 2.6 %collective-permute-start.3 = (bf16[8,144,128]{2,1,0:T(8,128)(2,1)S(1)}, bf16[8,144,128]{2,1,0:T(8,128)(2,1)S(1)}, u32[]{:S(2)}, u32[]{:S(2)}) collective-permute-start(bf16[8,144,128]{2,1,0:T(8,128)(2,1)S(1)} %all_to_all.20.q0_ref), channel_id=1, source_target_pairs={{0,16},{8,24},{16,0},{24,8},{1,17},{9,25},{17,1},{25,9},{2,18},{10... | collective-permute-start | bytes 884744 | tf_op jit(solution)/shard_map/ppermute | solution.py:358
  25.5 1.1 %collective-permute-start.4 = (bf16[8,144,128]{2,1,0:T(8,128)(2,1)S(1)}, bf16[8,144,128]{2,1,0:T(8,128)(2,1)}, u32[]{:S(2)}, u32[]{:S(2)}) collective-permute-start(bf16[8,144,128]{2,1,0:T(8,128)(2,1)S(1)} %all_to_all.20.q0_ref), channel_id=1, source_target_pairs={{0,24},{8,0},{16,8},{24,16},{1,25},{9,1},{17,9},{25,17},{2,26},{10... | collective-permute-start | bytes 884744 | tf_op jit(solution)/shard_map/ppermute | solution.py:358
  26.6 0.8 concatenate.3.facts_ref
  27.4 0.0 collective-permute-done.peer_in
  27.4 0.0 copy-start
  27.4 2.2 %copy-done = bf16[32,512,128]{2,1,0:T(8,128)(2,1)S(1)} copy-done((bf16[32,512,128]{2,1,0:T(8,128)(2,1)S(1)}, bf16[32,512,128]{2,1,0:T(8,128)(2,1)}, u32[]{:S(2)}) %copy-start) | copy-done | bytes 4194328
  29.6 0.0 copy-start.2
  29.6 1.7 %copy-done.2 = bf16[64,32,576]{2,1,0:T(8,128)(2,1)S(1)} copy-done((bf16[64,32,576]{2,1,0:T(8,128)(2,1)S(1)}, bf16[64,32,576]{2,1,0:T(8,128)(2,1)}, u32[]{:S(2)}) %copy-start.2) | copy-done | bytes 2359320
  31.3 0.0 copy-start.3
  31.3 1.7 %copy-done.3 = bf16[2,1024,576]{1,2,0:T(8,128)(2,1)S(1)} copy-done((bf16[2,1024,576]{1,2,0:T(8,128)(2,1)S(1)}, bf16[2,1024,576]{1,2,0:T(8,128)(2,1)}, u32[]{:S(2)}) %copy-start.3) | copy-done | bytes 2359320
  33.0 0.0 copy-start.1
  33.0 0.0 copy-start.4
  33.0 3.1 %shard_map.74 = (s32[80]{0:T(128)S(1)}, bf16[9,256,576]{2,1,0:T(8,128)(2,1)S(1)}, bf16[2,576,1024]{2,1,0:T(8,128)(2,1)S(1)}) custom-call(s32[136]{0:T(256)S(1)} %concatenate.3.facts_ref, bf16[2,576,1024]{2,1,0:T(8,128)(2,1)S(1)} %bitcast.9, bf16[2,576,1024]{2,1,0:T(8,128)(2,1)} %collective-permute-done.peer_in, bf16[32,512,128]{2,1,0:T(8,128)(2,1)S(1)} %copy-done, ...), custom_call_target="tpu_custom_call" | custom-call | flops 268435456 | bytes 4194304 | tf_op jit(solution)/shard_map/pallas_call | solution.py:32
  36.1 0.0 collective-permute-done.2.q1_ref
  36.1 0.6 collective-permute-done.3.q2_ref
  36.7 0.1 collective-permute-done.4.q3_ref
  36.8 0.0 copy-done.1
  36.8 0.0 copy-done.4
  36.8 0.0 copy-start.5
  36.8 12.7 %shard_map.75 = bf16[32,40,128]{2,1,0:T(8,128)(2,1)S(1)} custom-call(s32[136]{0:T(256)S(1)} %concatenate.3.facts_ref, s32[80]{0:T(128)S(1)} %get-tuple-element.18.table_ref, bf16[8,144,128]{2,1,0:T(8,128)(2,1)S(1)} %all_to_all.20.q0_ref, bf16[8,144,128]{2,1,0:T(8,128)(2,1)S(1)} %collective-permute-done.2.q1_ref, ...), custom_call_target="tpu_custom_call" | custom-call | flops 6127616000 | bytes 4194304 | tf_op jit(solution)/shard_map/pallas_call | solution.py:32
  49.5 19.2 %all_to_all.21.got_ref = bf16[32,40,128]{2,1,0:T(8,128)(2,1)S(1)} all-to-all(bf16[32,40,128]{2,1,0:T(8,128)(2,1)S(1)} %shard_map.75), channel_id=1, replica_groups=mesh['z'=8,'y'=4,'c'=2,'x'=4] {'z','y'}, dimensions={0} | all-to-all | bytes 655360 | tf_op jit(solution)/shard_map/all_to_all | solution.py:363
  68.7 1.0 shard_map.76
  69.7 0.0 copy-done.5
  69.7 2.9 %collective-permute-start.5 = (bf16[112,4096]{1,0:T(8,128)(2,1)S(1)}, bf16[112,4096]{1,0:T(8,128)(2,1)S(1)}, u32[]{:S(2)}, u32[]{:S(2)}) collective-permute-start(bf16[112,4096]{1,0:T(8,128)(2,1)S(1)} %bitcast.11), channel_id=1, source_target_pairs={{0,4},{4,0},{1,5},{5,1},{2,6},{6,2},{3,7},{7,3},{8,12},{12,8},{9,1... | collective-permute-start | bytes 2752520 | tf_op jit(solution)/shard_map/ppermute | solution.py:344
  72.6 15.7 %all_to_all.22.values_ref = bf16[32,32,128]{2,1,0:T(8,128)(2,1)S(1)} all-to-all(bf16[32,32,128]{2,1,0:T(8,128)(2,1)S(1)} %shard_map.76), channel_id=1, replica_groups=mesh['z'=8,'y'=4,'c'=2,'x'=4] {'z','y'}, dimensions={0} | all-to-all | bytes 524288 | tf_op jit(solution)/shard_map/all_to_all | solution.py:366
  88.3 0.0 collective-permute-done.5.peer_ref
  88.3 1.3 %shard_map.77 = f32[8,8,128]{2,1,0:T(8,128)S(1)} custom-call(s32[136]{0:T(256)S(1)} %concatenate.3.facts_ref, bf16[32,32,128]{2,1,0:T(8,128)(2,1)S(1)} %all_to_all.22.values_ref, bf16[112,4096]{1,0:T(8,128)(2,1)S(1)} %bitcast.12, bf16[112,4096]{1,0:T(8,128)(2,1)S(1)} %collective-permute-done.5.peer_ref), custom_call_target="tpu_custom_call" | custom-call | flops 134217728 | bytes 4194304 | tf_op jit(solution)/shard_map/pallas_call | solution.py:32
  89.7 11.0 %all_to_all.23.got_ref = f32[8,8,128]{2,1,0:T(8,128)S(1)} all-to-all(f32[8,8,128]{2,1,0:T(8,128)S(1)} %shard_map.77), channel_id=1, replica_groups=mesh['z'=8,'y'=4,'c'=2,'x'=4] {'c','x'}, dimensions={0} | all-to-all | bytes 65536 | tf_op jit(solution)/shard_map/all_to_all | solution.py:368
  100.7 0.9 shard_map.78
  (1 shorter events, 0.0 us)
Async XLA Ops:
  0.0 21.6 %collective-permute-start.1 = (bf16[64,32,576]{2,1,0:T(8,128)(2,1)}, bf16[64,32,576]{2,1,0:T(8,128)(2,1)S(1)}, u32[]{:S(2)}, u32[]{:S(2)}) collective-permute-start(bf16[64,32,576]{2,1,0:T(8,128)(2,1)} %suf_own_ref.1), channel_id=1, source_target_pairs={{0,4},{4,0},{1,5},{5,1},{2,6},{6,2},{3,7},{7,3},{8,12},{12,8},{9,1... | collective-permute-start | bytes 7077896 | tf_op jit(solution)/shard_map/ppermute | solution.py:344
  3.2 24.1 %collective-permute-start = (bf16[2,576,1024]{2,1,0:T(8,128)(2,1)}, bf16[2,576,1024]{2,1,0:T(8,128)(2,1)}, u32[]{:S(2)}, u32[]{:S(2)}) collective-permute-start(bf16[2,576,1024]{2,1,0:T(8,128)(2,1)} %bitcast.8), channel_id=1, source_target_pairs={{0,4},{4,0},{1,5},{5,1},{2,6},{6,2},{3,7},{7,3},{8,12},{12,8},{9,1... | collective-permute-start | bytes 7077896 | tf_op jit(solution)/shard_map/ppermute | solution.py:344
  3.2 0.8 copy-start.6
  21.6 14.4 %collective-permute-start.2 = (bf16[8,144,128]{2,1,0:T(8,128)(2,1)S(1)}, bf16[8,144,128]{2,1,0:T(8,128)(2,1)S(1)}, u32[]{:S(2)}, u32[]{:S(2)}) collective-permute-start(bf16[8,144,128]{2,1,0:T(8,128)(2,1)S(1)} %all_to_all.20.q0_ref), channel_id=1, source_target_pairs={{0,8},{8,16},{16,24},{24,0},{1,9},{9,17},{17,25},{25,1},{2,10},{10... | collective-permute-start | bytes 884744 | tf_op jit(solution)/shard_map/ppermute | solution.py:358
  22.9 13.7 %collective-permute-start.3 = (bf16[8,144,128]{2,1,0:T(8,128)(2,1)S(1)}, bf16[8,144,128]{2,1,0:T(8,128)(2,1)S(1)}, u32[]{:S(2)}, u32[]{:S(2)}) collective-permute-start(bf16[8,144,128]{2,1,0:T(8,128)(2,1)S(1)} %all_to_all.20.q0_ref), channel_id=1, source_target_pairs={{0,16},{8,24},{16,0},{24,8},{1,17},{9,25},{17,1},{25,9},{2,18},{10... | collective-permute-start | bytes 884744 | tf_op jit(solution)/shard_map/ppermute | solution.py:358
  25.5 11.3 %collective-permute-start.4 = (bf16[8,144,128]{2,1,0:T(8,128)(2,1)S(1)}, bf16[8,144,128]{2,1,0:T(8,128)(2,1)}, u32[]{:S(2)}, u32[]{:S(2)}) collective-permute-start(bf16[8,144,128]{2,1,0:T(8,128)(2,1)S(1)} %all_to_all.20.q0_ref), channel_id=1, source_target_pairs={{0,24},{8,0},{16,8},{24,16},{1,25},{9,1},{17,9},{25,17},{2,26},{10... | collective-permute-start | bytes 884744 | tf_op jit(solution)/shard_map/ppermute | solution.py:358
  27.4 2.2 %copy-start = (bf16[32,512,128]{2,1,0:T(8,128)(2,1)S(1)}, bf16[32,512,128]{2,1,0:T(8,128)(2,1)}, u32[]{:S(2)}) copy-start(bf16[32,512,128]{2,1,0:T(8,128)(2,1)} %uv_ref.1) | copy-start | bytes 12582916
  29.6 1.7 %copy-start.2 = (bf16[64,32,576]{2,1,0:T(8,128)(2,1)S(1)}, bf16[64,32,576]{2,1,0:T(8,128)(2,1)}, u32[]{:S(2)}) copy-start(bf16[64,32,576]{2,1,0:T(8,128)(2,1)} %suf_own_ref.1) | copy-start | bytes 7077892
  31.3 1.7 %copy-start.3 = (bf16[2,1024,576]{1,2,0:T(8,128)(2,1)S(1)}, bf16[2,1024,576]{1,2,0:T(8,128)(2,1)}, u32[]{:S(2)}) copy-start(bf16[2,1024,576]{1,2,0:T(8,128)(2,1)} %param.8) | copy-start | bytes 7077892
  33.0 3.8 %copy-start.1 = (bf16[32,512,128]{2,1,0:T(8,128)(2,1)S(1)}, bf16[32,512,128]{2,1,0:T(8,128)(2,1)}, u32[]{:S(2)}) copy-start(bf16[32,512,128]{2,1,0:T(8,128)(2,1)} %uv_ref.1) | copy-start | bytes 12582916
  33.0 3.8 %copy-start.4 = (bf16[2,1024,576]{1,2,0:T(8,128)(2,1)S(1)}, bf16[2,1024,576]{1,2,0:T(8,128)(2,1)}, u32[]{:S(2)}) copy-start(bf16[2,1024,576]{1,2,0:T(8,128)(2,1)} %param.8) | copy-start | bytes 7077892
  36.8 32.9 %copy-start.5 = (bf16[4096,112]{0,1:T(8,128)(2,1)S(1)}, bf16[4096,112]{0,1:T(8,128)(2,1)}, u32[]{:S(2)}) copy-start(bf16[4096,112]{0,1:T(8,128)(2,1)} %param.13) | copy-start | bytes 2752516
  69.7 18.6 %collective-permute-start.5 = (bf16[112,4096]{1,0:T(8,128)(2,1)S(1)}, bf16[112,4096]{1,0:T(8,128)(2,1)S(1)}, u32[]{:S(2)}, u32[]{:S(2)}) collective-permute-start(bf16[112,4096]{1,0:T(8,128)(2,1)S(1)} %bitcast.11), channel_id=1, source_target_pairs={{0,4},{4,0},{1,5},{5,1},{2,6},{6,2},{3,7},{7,3},{8,12},{12,8},{9,1... | collective-permute-start | bytes 2752520 | tf_op jit(solution)/shard_map/ppermute | solution.py:344

commit v6 on v4

--- a/solution.py
+++ b/solution.py
@@ -353,14 +353,13 @@
     own = jnp.transpose(prompt_cache, (0, 2, 1))
     peer, suf_peer = swap(own), swap(suffix_cache)
     along_z = lax.all_to_all(pack(queries), "z", 0, 0, tiled=True)
-    along_z, suf_peer = lax.optimization_barrier((along_z, suf_peer))
+    along_z, suf_peer, w_t = lax.optimization_barrier((along_z, suf_peer, w_out.T))
     qs = [along_z] + [
         lax.ppermute(along_z, "y", [(i, (i + j) % NY) for i in range(NY)]) for j in range(1, NY)
     ]
     table, keys, peer = prepare(facts, own, peer, w_uv, suffix_cache, suf_peer)
-    qs, keys, w_t = lax.optimization_barrier((qs, keys, w_out.T))
+    qs, keys, w_peer = lax.optimization_barrier((qs, keys, swap(w_t)))
     parts = attend(facts, table, qs, own, peer, keys, w_uv)
-    parts, w_peer = lax.optimization_barrier((parts, swap(w_t)))
     got = lax.all_to_all(parts, ("z", "y"), 0, 0, tiled=True)
     values = lax.all_to_all(combine(facts, got), ("z", "y"), 0, 0, tiled=True)
     shares = project(facts, values, w_t, w_peer)

time: 101 us -> 102 us (level)
  waiting for transfers between devices: 0.74 us -> 3.29 us
  blocking collectives: 62.9 us -> 61.4 us
    all_to_all x1, blocking collectives: 18.2 us -> 15.6 us  [per_device(): got = lax.all_to_all(parts, ('z', 'y'), 0, 0, tiled=True)]
    ppermute x3, waiting for transfers between devices: 0.73 us -> 3.28 us  [per_device(): lax.ppermute(along_z, 'y', [(i, (i + j) % NY) for i in range(NY)])]
  transfers between devices with their start and end apart: 6 -> 6, of which waited for: 2 -> 1; matrix products, arithmetic and copies ran while one was open for 1% -> 1% of each run, Pallas kernels for 16% -> 3%
where the time goes in v6:
time: 102 us
  blocking collectives  61.4 us (60%)
  Pallas kernels  19.3 us (19%)
  starting transfers between devices  10.5 us (10%)
  local copies, waits for them, and re-layouts  7.13 us (7%)
  waiting for transfers between devices  3.29 us (3%)
    pallas_call x6, Pallas kernels, call(): pl.pallas_call(kernel, out_shape=out, in_specs=specs, out_specs=out_specs...  19.3 us
    all_to_all x1, blocking collectives, per_device(): along_z = lax.all_to_all(pack(queries), 'z', 0, 0, tiled=True)  17.6 us
    all_to_all x1, blocking collectives, per_device(): got = lax.all_to_all(parts, ('z', 'y'), 0, 0, tiled=True)  15.6 us
    all_to_all x1, blocking collectives, per_device(): values = lax.all_to_all(combine(facts, got), ('z', 'y'), 0, 0, tiled=True)  15.3 us
    all_to_all x1, blocking collectives, per_device(): return finish(lax.all_to_all(shares, ('c', 'x'), 0, 0, tiled=True)).T  12.8 us
    unnamed x14, local copies, waits for them, and re-layouts  6.38 us
    ppermute x3, starting transfers between devices, swap(): return lax.ppermute(x, 'c', [(0, 1), (1, 0)])  5.49 us
    ppermute x3, starting transfers between devices, per_device(): lax.ppermute(along_z, 'y', [(i, (i + j) % NY) for i in range(NY)])  4.99 us
  transfers between devices with their start and end apart: 6, of which 1 were waited for; matrix products, arithmetic and copies ran while one was open for 1% of the time, Pallas kernels for 3%

profile of v6, /device:TPU:1, one launch (start us, length us, event | category | flops | bytes accessed | tf_op | source)
XLA Modules:
  0.0 101.7 jit_solution(14889702168711751592)
XLA Ops:
  0.0 3.2 %collective-permute-start.1 = (bf16[64,32,576]{2,1,0:T(8,128)(2,1)}, bf16[64,32,576]{2,1,0:T(8,128)(2,1)S(1)}, u32[]{:S(2)}, u32[]{:S(2)}) collective-permute-start(bf16[64,32,576]{2,1,0:T(8,128)(2,1)} %suf_own_ref.1), channel_id=1, source_target_pairs={{0,4},{4,0},{1,5},{5,1},{2,6},{6,2},{3,7},{7,3},{8,12},{12,8},{9,1... | collective-permute-start | bytes 7077896 | tf_op jit(solution)/shard_map/ppermute | solution.py:344
  3.2 0.0 collective-permute-start
  3.2 0.0 copy-start.6
  3.2 0.8 copy-done.6
  4.0 0.1 shard_map.73
  4.1 17.6 %all_to_all.20.q0_ref = bf16[8,144,128]{2,1,0:T(8,128)(2,1)} all-to-all(bf16[8,144,128]{2,1,0:T(8,128)(2,1)S(1)} %shard_map.73), channel_id=1, replica_groups=mesh['z'=8,'y'=4,'c'=2,'x'=4] {'z'}, dimensions={0} | all-to-all | bytes 589824 | tf_op jit(solution)/shard_map/all_to_all | solution.py:355
  21.7 0.0 collective-permute-done.1.suf_peer_ref
  21.7 2.2 %collective-permute-start.5 = (bf16[112,4096]{1,0:T(8,128)(2,1)}, bf16[112,4096]{1,0:T(8,128)(2,1)S(1)}, u32[]{:S(2)}, u32[]{:S(2)}) collective-permute-start(bf16[112,4096]{1,0:T(8,128)(2,1)} %bitcast.11), channel_id=1, source_target_pairs={{0,4},{4,0},{1,5},{5,1},{2,6},{6,2},{3,7},{7,3},{8,12},{12,8},{9,1... | collective-permute-start | bytes 2752520 | tf_op jit(solution)/shard_map/ppermute | solution.py:344
  24.0 1.3 %collective-permute-start.2 = (bf16[8,144,128]{2,1,0:T(8,128)(2,1)}, bf16[8,144,128]{2,1,0:T(8,128)(2,1)}, u32[]{:S(2)}, u32[]{:S(2)}) collective-permute-start(bf16[8,144,128]{2,1,0:T(8,128)(2,1)} %all_to_all.20.q0_ref), channel_id=1, source_target_pairs={{0,8},{8,16},{16,24},{24,0},{1,9},{9,17},{17,25},{25,1},{2,10},{10... | collective-permute-start | bytes 884744 | tf_op jit(solution)/shard_map/ppermute | solution.py:358
  25.3 2.6 %collective-permute-start.3 = (bf16[8,144,128]{2,1,0:T(8,128)(2,1)}, bf16[8,144,128]{2,1,0:T(8,128)(2,1)}, u32[]{:S(2)}, u32[]{:S(2)}) collective-permute-start(bf16[8,144,128]{2,1,0:T(8,128)(2,1)} %all_to_all.20.q0_ref), channel_id=1, source_target_pairs={{0,16},{8,24},{16,0},{24,8},{1,17},{9,25},{17,1},{25,9},{2,18},{10... | collective-permute-start | bytes 884744 | tf_op jit(solution)/shard_map/ppermute | solution.py:358
  27.9 1.1 %collective-permute-start.4 = (bf16[8,144,128]{2,1,0:T(8,128)(2,1)}, bf16[8,144,128]{2,1,0:T(8,128)(2,1)}, u32[]{:S(2)}, u32[]{:S(2)}) collective-permute-start(bf16[8,144,128]{2,1,0:T(8,128)(2,1)} %all_to_all.20.q0_ref), channel_id=1, source_target_pairs={{0,24},{8,0},{16,8},{24,16},{1,25},{9,1},{17,9},{25,17},{2,26},{10... | collective-permute-start | bytes 884744 | tf_op jit(solution)/shard_map/ppermute | solution.py:358
  29.0 0.8 concatenate.3.facts_ref
  29.7 0.0 collective-permute-done.peer_in
  29.7 0.0 copy-start
  29.7 2.2 %copy-done = bf16[32,512,128]{2,1,0:T(8,128)(2,1)S(1)} copy-done((bf16[32,512,128]{2,1,0:T(8,128)(2,1)S(1)}, bf16[32,512,128]{2,1,0:T(8,128)(2,1)}, u32[]{:S(2)}) %copy-start) | copy-done | bytes 4194328
  31.9 0.0 copy-start.2
  31.9 1.7 %copy-done.2 = bf16[64,32,576]{2,1,0:T(8,128)(2,1)S(1)} copy-done((bf16[64,32,576]{2,1,0:T(8,128)(2,1)S(1)}, bf16[64,32,576]{2,1,0:T(8,128)(2,1)}, u32[]{:S(2)}) %copy-start.2) | copy-done | bytes 2359320
  33.7 0.0 copy-start.3
  33.7 1.7 %copy-done.3 = bf16[2,1024,576]{1,2,0:T(8,128)(2,1)S(1)} copy-done((bf16[2,1024,576]{1,2,0:T(8,128)(2,1)S(1)}, bf16[2,1024,576]{1,2,0:T(8,128)(2,1)}, u32[]{:S(2)}) %copy-start.3) | copy-done | bytes 2359320
  35.3 0.0 copy-start.1
  35.3 0.0 copy-start.4
  35.3 3.1 %shard_map.74 = (s32[80]{0:T(128)S(1)}, bf16[9,256,576]{2,1,0:T(8,128)(2,1)S(1)}, bf16[2,576,1024]{2,1,0:T(8,128)(2,1)S(1)}) custom-call(s32[136]{0:T(256)S(1)} %concatenate.3.facts_ref, bf16[2,576,1024]{2,1,0:T(8,128)(2,1)S(1)} %bitcast.9, bf16[2,576,1024]{2,1,0:T(8,128)(2,1)} %collective-permute-done.peer_in, bf16[32,512,128]{2,1,0:T(8,128)(2,1)S(1)} %copy-done, ...), custom_call_target="tpu_custom_call" | custom-call | flops 268435456 | bytes 4194304 | tf_op jit(solution)/shard_map/pallas_call | solution.py:32
  38.4 0.0 collective-permute-done.2.q1_ref
  38.4 3.3 %collective-permute-done.3.q2_ref = bf16[8,144,128]{2,1,0:T(8,128)(2,1)} collective-permute-done((bf16[8,144,128]{2,1,0:T(8,128)(2,1)}, bf16[8,144,128]{2,1,0:T(8,128)(2,1)}, u32[]{:S(2)}, u32[]{:S(2)}) %collective-permute-start.3) | collective-permute-done | bytes 294944 | tf_op jit(solution)/shard_map/ppermute | solution.py:358
  41.7 0.0 collective-permute-done.4.q3_ref
  41.7 0.0 collective-permute-done.5.peer_ref
  41.7 0.0 copy-done.1
  41.7 0.0 copy-done.4
  41.7 0.0 copy-start.5
  41.7 13.0 %shard_map.75 = bf16[32,40,128]{2,1,0:T(8,128)(2,1)S(1)} custom-call(s32[136]{0:T(256)S(1)} %concatenate.3.facts_ref, s32[80]{0:T(128)S(1)} %get-tuple-element.18.table_ref, bf16[8,144,128]{2,1,0:T(8,128)(2,1)} %all_to_all.20.q0_ref, bf16[8,144,128]{2,1,0:T(8,128)(2,1)} %collective-permute-done.2.q1_ref, bf16[8,144,128]{2,1,0:T(8,128)(2,1)} %collective-permute-done.3.q2_ref, ...), custom_call_target="tpu_custom_call" | custom-call | flops 6127616000 | bytes 4194304 | tf_op jit(solution)/shard_map/pallas_call | solution.py:32
  54.7 15.6 %all_to_all.21.got_ref = bf16[32,40,128]{2,1,0:T(8,128)(2,1)S(1)} all-to-all(bf16[32,40,128]{2,1,0:T(8,128)(2,1)S(1)} %shard_map.75), channel_id=1, replica_groups=mesh['z'=8,'y'=4,'c'=2,'x'=4] {'z','y'}, dimensions={0} | all-to-all | bytes 655360 | tf_op jit(solution)/shard_map/all_to_all | solution.py:363
  70.3 1.0 shard_map.76
  71.4 15.3 %all_to_all.22.values_ref = bf16[32,32,128]{2,1,0:T(8,128)(2,1)S(1)} all-to-all(bf16[32,32,128]{2,1,0:T(8,128)(2,1)S(1)} %shard_map.76), channel_id=1, replica_groups=mesh['z'=8,'y'=4,'c'=2,'x'=4] {'z','y'}, dimensions={0} | all-to-all | bytes 524288 | tf_op jit(solution)/shard_map/all_to_all | solution.py:364
  86.7 0.0 copy-done.5
  86.7 1.3 %shard_map.77 = f32[8,8,128]{2,1,0:T(8,128)S(1)} custom-call(s32[136]{0:T(256)S(1)} %concatenate.3.facts_ref, bf16[32,32,128]{2,1,0:T(8,128)(2,1)S(1)} %all_to_all.22.values_ref, bf16[112,4096]{1,0:T(8,128)(2,1)S(1)} %bitcast.12, bf16[112,4096]{1,0:T(8,128)(2,1)S(1)} %collective-permute-done.5.peer_ref), custom_call_target="tpu_custom_call" | custom-call | flops 134217728 | bytes 4194304 | tf_op jit(solution)/shard_map/pallas_call | solution.py:32
  88.0 12.8 %all_to_all.23.got_ref = f32[8,8,128]{2,1,0:T(8,128)S(1)} all-to-all(f32[8,8,128]{2,1,0:T(8,128)S(1)} %shard_map.77), channel_id=1, replica_groups=mesh['z'=8,'y'=4,'c'=2,'x'=4] {'c','x'}, dimensions={0} | all-to-all | bytes 65536 | tf_op jit(solution)/shard_map/all_to_all | solution.py:366
  100.8 0.9 shard_map.78
  (1 shorter events, 0.0 us)
Async XLA Ops:
  0.0 21.7 %collective-permute-start.1 = (bf16[64,32,576]{2,1,0:T(8,128)(2,1)}, bf16[64,32,576]{2,1,0:T(8,128)(2,1)S(1)}, u32[]{:S(2)}, u32[]{:S(2)}) collective-permute-start(bf16[64,32,576]{2,1,0:T(8,128)(2,1)} %suf_own_ref.1), channel_id=1, source_target_pairs={{0,4},{4,0},{1,5},{5,1},{2,6},{6,2},{3,7},{7,3},{8,12},{12,8},{9,1... | collective-permute-start | bytes 7077896 | tf_op jit(solution)/shard_map/ppermute | solution.py:344
  3.2 26.5 %collective-permute-start = (bf16[2,576,1024]{2,1,0:T(8,128)(2,1)}, bf16[2,576,1024]{2,1,0:T(8,128)(2,1)}, u32[]{:S(2)}, u32[]{:S(2)}) collective-permute-start(bf16[2,576,1024]{2,1,0:T(8,128)(2,1)} %bitcast.8), channel_id=1, source_target_pairs={{0,4},{4,0},{1,5},{5,1},{2,6},{6,2},{3,7},{7,3},{8,12},{12,8},{9,1... | collective-permute-start | bytes 7077896 | tf_op jit(solution)/shard_map/ppermute | solution.py:344
  3.2 0.8 copy-start.6
  21.7 20.0 %collective-permute-start.5 = (bf16[112,4096]{1,0:T(8,128)(2,1)}, bf16[112,4096]{1,0:T(8,128)(2,1)S(1)}, u32[]{:S(2)}, u32[]{:S(2)}) collective-permute-start(bf16[112,4096]{1,0:T(8,128)(2,1)} %bitcast.11), channel_id=1, source_target_pairs={{0,4},{4,0},{1,5},{5,1},{2,6},{6,2},{3,7},{7,3},{8,12},{12,8},{9,1... | collective-permute-start | bytes 2752520 | tf_op jit(solution)/shard_map/ppermute | solution.py:344
  24.0 14.4 %collective-permute-start.2 = (bf16[8,144,128]{2,1,0:T(8,128)(2,1)}, bf16[8,144,128]{2,1,0:T(8,128)(2,1)}, u32[]{:S(2)}, u32[]{:S(2)}) collective-permute-start(bf16[8,144,128]{2,1,0:T(8,128)(2,1)} %all_to_all.20.q0_ref), channel_id=1, source_target_pairs={{0,8},{8,16},{16,24},{24,0},{1,9},{9,17},{17,25},{25,1},{2,10},{10... | collective-permute-start | bytes 884744 | tf_op jit(solution)/shard_map/ppermute | solution.py:358
  25.3 16.4 %collective-permute-start.3 = (bf16[8,144,128]{2,1,0:T(8,128)(2,1)}, bf16[8,144,128]{2,1,0:T(8,128)(2,1)}, u32[]{:S(2)}, u32[]{:S(2)}) collective-permute-start(bf16[8,144,128]{2,1,0:T(8,128)(2,1)} %all_to_all.20.q0_ref), channel_id=1, source_target_pairs={{0,16},{8,24},{16,0},{24,8},{1,17},{9,25},{17,1},{25,9},{2,18},{10... | collective-permute-start | bytes 884744 | tf_op jit(solution)/shard_map/ppermute | solution.py:358
  27.9 13.8 %collective-permute-start.4 = (bf16[8,144,128]{2,1,0:T(8,128)(2,1)}, bf16[8,144,128]{2,1,0:T(8,128)(2,1)}, u32[]{:S(2)}, u32[]{:S(2)}) collective-permute-start(bf16[8,144,128]{2,1,0:T(8,128)(2,1)} %all_to_all.20.q0_ref), channel_id=1, source_target_pairs={{0,24},{8,0},{16,8},{24,16},{1,25},{9,1},{17,9},{25,17},{2,26},{10... | collective-permute-start | bytes 884744 | tf_op jit(solution)/shard_map/ppermute | solution.py:358
  29.7 2.2 %copy-start = (bf16[32,512,128]{2,1,0:T(8,128)(2,1)S(1)}, bf16[32,512,128]{2,1,0:T(8,128)(2,1)}, u32[]{:S(2)}) copy-start(bf16[32,512,128]{2,1,0:T(8,128)(2,1)} %uv_ref.1) | copy-start | bytes 12582916
  31.9 1.7 %copy-start.2 = (bf16[64,32,576]{2,1,0:T(8,128)(2,1)S(1)}, bf16[64,32,576]{2,1,0:T(8,128)(2,1)}, u32[]{:S(2)}) copy-start(bf16[64,32,576]{2,1,0:T(8,128)(2,1)} %suf_own_ref.1) | copy-start | bytes 7077892
  33.7 1.7 %copy-start.3 = (bf16[2,1024,576]{1,2,0:T(8,128)(2,1)S(1)}, bf16[2,1024,576]{1,2,0:T(8,128)(2,1)}, u32[]{:S(2)}) copy-start(bf16[2,1024,576]{1,2,0:T(8,128)(2,1)} %param.8) | copy-start | bytes 7077892
  35.3 6.4 %copy-start.1 = (bf16[32,512,128]{2,1,0:T(8,128)(2,1)S(1)}, bf16[32,512,128]{2,1,0:T(8,128)(2,1)}, u32[]{:S(2)}) copy-start(bf16[32,512,128]{2,1,0:T(8,128)(2,1)} %uv_ref.1) | copy-start | bytes 12582916
  35.3 6.4 %copy-start.4 = (bf16[2,1024,576]{1,2,0:T(8,128)(2,1)S(1)}, bf16[2,1024,576]{1,2,0:T(8,128)(2,1)}, u32[]{:S(2)}) copy-start(bf16[2,1024,576]{1,2,0:T(8,128)(2,1)} %param.8) | copy-start | bytes 7077892
  41.7 45.0 %copy-start.5 = (bf16[4096,112]{0,1:T(8,128)(2,1)S(1)}, bf16[4096,112]{0,1:T(8,128)(2,1)}, u32[]{:S(2)}) copy-start(bf16[4096,112]{0,1:T(8,128)(2,1)} %param.13) | copy-start | bytes 2752516

commit v7 on v4

--- a/solution.py
+++ b/solution.py
@@ -197,9 +197,9 @@
         )
 
     border = first // TILE * TILE
-    tile(CHIPS, SPARE, jnp.where(first - border <= SPARE, 0, 1))
     for i in range(CHIPS // TILE):
         tile(i * TILE, TILE, jnp.where(i * TILE + SPARE >= first, 1, 0))
+    tile(CHIPS, SPARE, jnp.where(first - border <= SPARE, 0, 1))
     for h in range(0, HEADS, 2):
         rows = jnp.concatenate(
             [

time: 101 us -> 101 us (level)
  no operation moved by 1% of the time
where the time goes in v7:
time: 101 us
  blocking collectives  62.9 us (62%)
  Pallas kernels  19 us (19%)
  starting transfers between devices  11.3 us (11%)
  local copies, waits for them, and re-layouts  7.13 us (7%)
    pallas_call x6, Pallas kernels, call(): pl.pallas_call(kernel, out_shape=out, in_specs=specs, out_specs=out_specs...  19 us
    all_to_all x1, blocking collectives, per_device(): got = lax.all_to_all(parts, ('z', 'y'), 0, 0, tiled=True)  18.3 us
    all_to_all x1, blocking collectives, per_device(): along_z = lax.all_to_all(pack(queries), 'z', 0, 0, tiled=True)  17.5 us
    all_to_all x1, blocking collectives, per_device(): values = lax.all_to_all(combine(facts, got), ('z', 'y'), 0, 0, tiled=True)  14.5 us
    all_to_all x1, blocking collectives, per_device(): return finish(lax.all_to_all(shares, ('c', 'x'), 0, 0, tiled=True)).T  12.6 us
    unnamed x14, local copies, waits for them, and re-layouts  6.38 us
    ppermute x3, starting transfers between devices, swap(): return lax.ppermute(x, 'c', [(0, 1), (1, 0)])  6.27 us
    ppermute x3, starting transfers between devices, per_device(): lax.ppermute(along_z, 'y', [(i, (i + j) % NY) for i in range(NY)])  4.99 us
  transfers between devices with their start and end apart: 6, of which 2 were waited for; matrix products, arithmetic and copies ran while one was open for 1% of the time, Pallas kernels for 16%

profile of v7, /device:TPU:1, one launch (start us, length us, event | category | flops | bytes accessed | tf_op | source)
XLA Modules:
  0.0 101.0 jit_solution(10895170826162790831)
XLA Ops:
  0.0 3.2 %collective-permute-start.1 = (bf16[64,32,576]{2,1,0:T(8,128)(2,1)}, bf16[64,32,576]{2,1,0:T(8,128)(2,1)S(1)}, u32[]{:S(2)}, u32[]{:S(2)}) collective-permute-start(bf16[64,32,576]{2,1,0:T(8,128)(2,1)} %suf_own_ref.1), channel_id=1, source_target_pairs={{0,4},{4,0},{1,5},{5,1},{2,6},{6,2},{3,7},{7,3},{8,12},{12,8},{9,1... | collective-permute-start | bytes 7077896 | tf_op jit(solution)/shard_map/ppermute | solution.py:344
  3.2 0.0 collective-permute-start
  3.2 0.0 copy-start.6
  3.2 0.8 copy-done.6
  4.0 0.1 shard_map.73
  4.1 17.5 %all_to_all.20.q0_ref = bf16[8,144,128]{2,1,0:T(8,128)(2,1)S(1)} all-to-all(bf16[8,144,128]{2,1,0:T(8,128)(2,1)S(1)} %shard_map.73), channel_id=1, replica_groups=mesh['z'=8,'y'=4,'c'=2,'x'=4] {'z'}, dimensions={0} | all-to-all | bytes 589824 | tf_op jit(solution)/shard_map/all_to_all | solution.py:355
  21.6 0.0 collective-permute-done.1.suf_peer_ref
  21.6 1.3 %collective-permute-start.2 = (bf16[8,144,128]{2,1,0:T(8,128)(2,1)S(1)}, bf16[8,144,128]{2,1,0:T(8,128)(2,1)S(1)}, u32[]{:S(2)}, u32[]{:S(2)}) collective-permute-start(bf16[8,144,128]{2,1,0:T(8,128)(2,1)S(1)} %all_to_all.20.q0_ref), channel_id=1, source_target_pairs={{0,8},{8,16},{16,24},{24,0},{1,9},{9,17},{17,25},{25,1},{2,10},{10... | collective-permute-start | bytes 884744 | tf_op jit(solution)/shard_map/ppermute | solution.py:358
  22.9 2.6 %collective-permute-start.3 = (bf16[8,144,128]{2,1,0:T(8,128)(2,1)S(1)}, bf16[8,144,128]{2,1,0:T(8,128)(2,1)S(1)}, u32[]{:S(2)}, u32[]{:S(2)}) collective-permute-start(bf16[8,144,128]{2,1,0:T(8,128)(2,1)S(1)} %all_to_all.20.q0_ref), channel_id=1, source_target_pairs={{0,16},{8,24},{16,0},{24,8},{1,17},{9,25},{17,1},{25,9},{2,18},{10... | collective-permute-start | bytes 884744 | tf_op jit(solution)/shard_map/ppermute | solution.py:358
  25.5 1.1 %collective-permute-start.4 = (bf16[8,144,128]{2,1,0:T(8,128)(2,1)S(1)}, bf16[8,144,128]{2,1,0:T(8,128)(2,1)}, u32[]{:S(2)}, u32[]{:S(2)}) collective-permute-start(bf16[8,144,128]{2,1,0:T(8,128)(2,1)S(1)} %all_to_all.20.q0_ref), channel_id=1, source_target_pairs={{0,24},{8,0},{16,8},{24,16},{1,25},{9,1},{17,9},{25,17},{2,26},{10... | collective-permute-start | bytes 884744 | tf_op jit(solution)/shard_map/ppermute | solution.py:358
  26.6 0.8 concatenate.3.facts_ref
  27.4 0.0 collective-permute-done.peer_in
  27.4 0.0 copy-start
  27.4 2.2 %copy-done = bf16[32,512,128]{2,1,0:T(8,128)(2,1)S(1)} copy-done((bf16[32,512,128]{2,1,0:T(8,128)(2,1)S(1)}, bf16[32,512,128]{2,1,0:T(8,128)(2,1)}, u32[]{:S(2)}) %copy-start) | copy-done | bytes 4194328
  29.6 0.0 copy-start.2
  29.6 1.7 %copy-done.2 = bf16[64,32,576]{2,1,0:T(8,128)(2,1)S(1)} copy-done((bf16[64,32,576]{2,1,0:T(8,128)(2,1)S(1)}, bf16[64,32,576]{2,1,0:T(8,128)(2,1)}, u32[]{:S(2)}) %copy-start.2) | copy-done | bytes 2359320
  31.3 0.0 copy-start.3
  31.3 1.7 %copy-done.3 = bf16[2,1024,576]{1,2,0:T(8,128)(2,1)S(1)} copy-done((bf16[2,1024,576]{1,2,0:T(8,128)(2,1)S(1)}, bf16[2,1024,576]{1,2,0:T(8,128)(2,1)}, u32[]{:S(2)}) %copy-start.3) | copy-done | bytes 2359320
  33.0 0.0 copy-start.5
  33.0 0.0 copy-start.1
  33.0 0.0 copy-start.4
  33.0 3.1 %shard_map.74 = (s32[80]{0:T(128)S(1)}, bf16[9,256,576]{2,1,0:T(8,128)(2,1)S(1)}, bf16[2,576,1024]{2,1,0:T(8,128)(2,1)S(1)}) custom-call(s32[136]{0:T(256)S(1)} %concatenate.3.facts_ref, bf16[2,576,1024]{2,1,0:T(8,128)(2,1)S(1)} %bitcast.9, bf16[2,576,1024]{2,1,0:T(8,128)(2,1)} %collective-permute-done.peer_in, bf16[32,512,128]{2,1,0:T(8,128)(2,1)S(1)} %copy-done, ...), custom_call_target="tpu_custom_call" | custom-call | flops 268435456 | bytes 4194304 | tf_op jit(solution)/shard_map/pallas_call | solution.py:32
  36.1 0.0 collective-permute-done.2.q1_ref
  36.1 0.6 collective-permute-done.3.q2_ref
  36.7 0.1 collective-permute-done.4.q3_ref
  36.8 0.0 copy-done.5
  36.8 3.0 %collective-permute-start.5 = (bf16[112,4096]{1,0:T(8,128)(2,1)S(1)}, bf16[112,4096]{1,0:T(8,128)(2,1)S(1)}, u32[]{:S(2)}, u32[]{:S(2)}) collective-permute-start(bf16[112,4096]{1,0:T(8,128)(2,1)S(1)} %bitcast.11), channel_id=1, source_target_pairs={{0,4},{4,0},{1,5},{5,1},{2,6},{6,2},{3,7},{7,3},{8,12},{12,8},{9,1... | collective-permute-start | bytes 2752520 | tf_op jit(solution)/shard_map/ppermute | solution.py:344
  39.8 0.0 copy-done.1
  39.8 0.0 copy-done.4
  39.8 12.6 %shard_map.75 = bf16[32,40,128]{2,1,0:T(8,128)(2,1)S(1)} custom-call(s32[136]{0:T(256)S(1)} %concatenate.3.facts_ref, s32[80]{0:T(128)S(1)} %get-tuple-element.19.table_ref, bf16[8,144,128]{2,1,0:T(8,128)(2,1)S(1)} %all_to_all.20.q0_ref, bf16[8,144,128]{2,1,0:T(8,128)(2,1)S(1)} %collective-permute-done.2.q1_ref, ...), custom_call_target="tpu_custom_call" | custom-call | flops 6127616000 | bytes 4194304 | tf_op jit(solution)/shard_map/pallas_call | solution.py:32
  52.4 0.0 collective-permute-done.5.peer_ref
  52.4 18.3 %all_to_all.21.got_ref = bf16[32,40,128]{2,1,0:T(8,128)(2,1)S(1)} all-to-all(bf16[32,40,128]{2,1,0:T(8,128)(2,1)S(1)} %shard_map.75), channel_id=1, replica_groups=mesh['z'=8,'y'=4,'c'=2,'x'=4] {'z','y'}, dimensions={0} | all-to-all | bytes 655360 | tf_op jit(solution)/shard_map/all_to_all | solution.py:364
  70.7 1.0 %shard_map.76 = bf16[32,32,128]{2,1,0:T(8,128)(2,1)S(1)} custom-call(s32[136]{0:T(256)S(1)} %concatenate.3.facts_ref, bf16[32,40,128]{2,1,0:T(8,128)(2,1)S(1)} %all_to_all.21.got_ref), custom_call_target="tpu_custom_call" | custom-call | flops 16777216 | bytes 4194304 | tf_op jit(solution)/shard_map/pallas_call | solution.py:32
  71.7 14.5 %all_to_all.22.values_ref = bf16[32,32,128]{2,1,0:T(8,128)(2,1)S(1)} all-to-all(bf16[32,32,128]{2,1,0:T(8,128)(2,1)S(1)} %shard_map.76), channel_id=1, replica_groups=mesh['z'=8,'y'=4,'c'=2,'x'=4] {'z','y'}, dimensions={0} | all-to-all | bytes 524288 | tf_op jit(solution)/shard_map/all_to_all | solution.py:365
  86.3 1.3 %shard_map.77 = f32[8,8,128]{2,1,0:T(8,128)S(1)} custom-call(s32[136]{0:T(256)S(1)} %concatenate.3.facts_ref, bf16[32,32,128]{2,1,0:T(8,128)(2,1)S(1)} %all_to_all.22.values_ref, bf16[112,4096]{1,0:T(8,128)(2,1)S(1)} %bitcast.12, bf16[112,4096]{1,0:T(8,128)(2,1)S(1)} %collective-permute-done.5.peer_ref), custom_call_target="tpu_custom_call" | custom-call | flops 134217728 | bytes 4194304 | tf_op jit(solution)/shard_map/pallas_call | solution.py:32
  87.6 12.6 %all_to_all.23.got_ref = f32[8,8,128]{2,1,0:T(8,128)S(1)} all-to-all(f32[8,8,128]{2,1,0:T(8,128)S(1)} %shard_map.77), channel_id=1, replica_groups=mesh['z'=8,'y'=4,'c'=2,'x'=4] {'c','x'}, dimensions={0} | all-to-all | bytes 65536 | tf_op jit(solution)/shard_map/all_to_all | solution.py:367
  100.2 0.9 shard_map.78
  (1 shorter events, 0.0 us)
Async XLA Ops:
  0.0 21.6 %collective-permute-start.1 = (bf16[64,32,576]{2,1,0:T(8,128)(2,1)}, bf16[64,32,576]{2,1,0:T(8,128)(2,1)S(1)}, u32[]{:S(2)}, u32[]{:S(2)}) collective-permute-start(bf16[64,32,576]{2,1,0:T(8,128)(2,1)} %suf_own_ref.1), channel_id=1, source_target_pairs={{0,4},{4,0},{1,5},{5,1},{2,6},{6,2},{3,7},{7,3},{8,12},{12,8},{9,1... | collective-permute-start | bytes 7077896 | tf_op jit(solution)/shard_map/ppermute | solution.py:344
  3.2 24.1 %collective-permute-start = (bf16[2,576,1024]{2,1,0:T(8,128)(2,1)}, bf16[2,576,1024]{2,1,0:T(8,128)(2,1)}, u32[]{:S(2)}, u32[]{:S(2)}) collective-permute-start(bf16[2,576,1024]{2,1,0:T(8,128)(2,1)} %bitcast.8), channel_id=1, source_target_pairs={{0,4},{4,0},{1,5},{5,1},{2,6},{6,2},{3,7},{7,3},{8,12},{12,8},{9,1... | collective-permute-start | bytes 7077896 | tf_op jit(solution)/shard_map/ppermute | solution.py:344
  3.2 0.8 copy-start.6
  21.6 14.4 %collective-permute-start.2 = (bf16[8,144,128]{2,1,0:T(8,128)(2,1)S(1)}, bf16[8,144,128]{2,1,0:T(8,128)(2,1)S(1)}, u32[]{:S(2)}, u32[]{:S(2)}) collective-permute-start(bf16[8,144,128]{2,1,0:T(8,128)(2,1)S(1)} %all_to_all.20.q0_ref), channel_id=1, source_target_pairs={{0,8},{8,16},{16,24},{24,0},{1,9},{9,17},{17,25},{25,1},{2,10},{10... | collective-permute-start | bytes 884744 | tf_op jit(solution)/shard_map/ppermute | solution.py:358
  22.9 13.7 %collective-permute-start.3 = (bf16[8,144,128]{2,1,0:T(8,128)(2,1)S(1)}, bf16[8,144,128]{2,1,0:T(8,128)(2,1)S(1)}, u32[]{:S(2)}, u32[]{:S(2)}) collective-permute-start(bf16[8,144,128]{2,1,0:T(8,128)(2,1)S(1)} %all_to_all.20.q0_ref), channel_id=1, source_target_pairs={{0,16},{8,24},{16,0},{24,8},{1,17},{9,25},{17,1},{25,9},{2,18},{10... | collective-permute-start | bytes 884744 | tf_op jit(solution)/shard_map/ppermute | solution.py:358
  25.5 11.3 %collective-permute-start.4 = (bf16[8,144,128]{2,1,0:T(8,128)(2,1)S(1)}, bf16[8,144,128]{2,1,0:T(8,128)(2,1)}, u32[]{:S(2)}, u32[]{:S(2)}) collective-permute-start(bf16[8,144,128]{2,1,0:T(8,128)(2,1)S(1)} %all_to_all.20.q0_ref), channel_id=1, source_target_pairs={{0,24},{8,0},{16,8},{24,16},{1,25},{9,1},{17,9},{25,17},{2,26},{10... | collective-permute-start | bytes 884744 | tf_op jit(solution)/shard_map/ppermute | solution.py:358
  27.4 2.2 %copy-start = (bf16[32,512,128]{2,1,0:T(8,128)(2,1)S(1)}, bf16[32,512,128]{2,1,0:T(8,128)(2,1)}, u32[]{:S(2)}) copy-start(bf16[32,512,128]{2,1,0:T(8,128)(2,1)} %uv_ref.1) | copy-start | bytes 12582916
  29.6 1.7 %copy-start.2 = (bf16[64,32,576]{2,1,0:T(8,128)(2,1)S(1)}, bf16[64,32,576]{2,1,0:T(8,128)(2,1)}, u32[]{:S(2)}) copy-start(bf16[64,32,576]{2,1,0:T(8,128)(2,1)} %suf_own_ref.1) | copy-start | bytes 7077892
  31.3 1.7 %copy-start.3 = (bf16[2,1024,576]{1,2,0:T(8,128)(2,1)S(1)}, bf16[2,1024,576]{1,2,0:T(8,128)(2,1)}, u32[]{:S(2)}) copy-start(bf16[2,1024,576]{1,2,0:T(8,128)(2,1)} %param.8) | copy-start | bytes 7077892
  33.0 3.8 %copy-start.5 = (bf16[4096,112]{0,1:T(8,128)(2,1)S(1)}, bf16[4096,112]{0,1:T(8,128)(2,1)}, u32[]{:S(2)}) copy-start(bf16[4096,112]{0,1:T(8,128)(2,1)} %param.13) | copy-start | bytes 2752516
  33.0 6.9 %copy-start.1 = (bf16[32,512,128]{2,1,0:T(8,128)(2,1)S(1)}, bf16[32,512,128]{2,1,0:T(8,128)(2,1)}, u32[]{:S(2)}) copy-start(bf16[32,512,128]{2,1,0:T(8,128)(2,1)} %uv_ref.1) | copy-start | bytes 12582916
  33.0 6.9 %copy-start.4 = (bf16[2,1024,576]{1,2,0:T(8,128)(2,1)S(1)}, bf16[2,1024,576]{1,2,0:T(8,128)(2,1)}, u32[]{:S(2)}) copy-start(bf16[2,1024,576]{1,2,0:T(8,128)(2,1)} %param.8) | copy-start | bytes 7077892
  36.8 15.6 %collective-permute-start.5 = (bf16[112,4096]{1,0:T(8,128)(2,1)S(1)}, bf16[112,4096]{1,0:T(8,128)(2,1)S(1)}, u32[]{:S(2)}, u32[]{:S(2)}) collective-permute-start(bf16[112,4096]{1,0:T(8,128)(2,1)S(1)} %bitcast.11), channel_id=1, source_target_pairs={{0,4},{4,0},{1,5},{5,1},{2,6},{6,2},{3,7},{7,3},{8,12},{12,8},{9,1... | collective-permute-start | bytes 2752520 | tf_op jit(solution)/shard_map/ppermute | solution.py:344
